TPU v7x, 32 devices: a whole 2x2x4 slice. The times are simulated.
32 devices in a mesh: dp: 2 (over y), fsdp: 16 (over z, x, core).
Axes of the slice: x: 2, y: 2, z: 4, core: 2. Of those that a mesh axis runs over, the one named last changes fastest.
Arguments:
- hidden: bfloat16 [64, 512, 768], P(('dp', 'fsdp')), may hold values from -6 to 6
- grad_out: bfloat16 [64, 512, 768], P(('dp', 'fsdp')), may hold values from -6 to 6
- past_states: bfloat16 [64, 512, 768], P(('dp', 'fsdp')), may hold values from -6 to 6
- old_coeffs: bfloat16 [64, 512, 768], P(('dp', 'fsdp')), may hold values from -6 to 6
- fresh_flags: int32 [64], P(('dp', 'fsdp')), may hold values 0 or 1
- ridge_map: bfloat16 [512, 1024], replicated, may hold values from -0.1875 to 0.1875
- gain_attn: bfloat16 [768], P(('dp', 'fsdp')), may hold values from 0.25 to 1.75
- shift_attn: bfloat16 [768], P(('dp', 'fsdp')), may hold values from -1.75 to 1.75
- qkv_weight: bfloat16 [768, 2304], P(('dp', 'fsdp')), may hold values from -0.21875 to 0.21875
- qv_bias: bfloat16 [1536], P(('dp', 'fsdp')), may hold values from -1.75 to 1.75
- out_weight: bfloat16 [768, 768], P(('dp', 'fsdp')), may hold values from -0.4375 to 0.4375
- out_bias: bfloat16 [768], P(('dp', 'fsdp')), may hold values from -1.75 to 1.75
- gain_mlp: bfloat16 [768], P(('dp', 'fsdp')), may hold values from 0.25 to 1.75
- shift_mlp: bfloat16 [768], P(('dp', 'fsdp')), may hold values from -1.75 to 1.75
- up_weight: bfloat16 [768, 3072], P(('dp', 'fsdp')), may hold values from -0.21875 to 0.21875
- up_bias: bfloat16 [3072], P(('dp', 'fsdp')), may hold values from -1.75 to 1.75
- down_weight: bfloat16 [3072, 768], P(('dp', 'fsdp')), may hold values from -0.109375 to 0.109375
- down_bias: bfloat16 [768], P(('dp', 'fsdp')), may hold values from -1.75 to 1.75
- mean_weight: bfloat16 [512, 12], P(('dp', 'fsdp')), may hold values from -0.25 to 0.25
- width_weight: bfloat16 [512, 12], P(('dp', 'fsdp')), may hold values from -0.25 to 0.25
Outputs:
- output: bfloat16 [64, 512, 768], P(('dp', 'fsdp'))
- grad_input: bfloat16 [64, 512, 768], P(('dp', 'fsdp'))
- grad_gain_attn: float32 [768], P(('dp', 'fsdp'))
- grad_shift_attn: float32 [768], P(('dp', 'fsdp'))
- grad_qkv_weight: float32 [768, 2304], P(('dp', 'fsdp'))
- grad_qv_bias: float32 [1536], P(('dp', 'fsdp'))
- grad_out_weight: float32 [768, 768], P(('dp', 'fsdp'))
- grad_out_bias: float32 [768], P(('dp', 'fsdp'))
- grad_gain_mlp: float32 [768], P(('dp', 'fsdp'))
- grad_shift_mlp: float32 [768], P(('dp', 'fsdp'))
- grad_up_weight: float32 [768, 3072], P(('dp', 'fsdp'))
- grad_up_bias: float32 [3072], P(('dp', 'fsdp'))
- grad_down_weight: float32 [3072, 768], P(('dp', 'fsdp'))
- grad_down_bias: float32 [768], P(('dp', 'fsdp'))
- grad_mean_weight: float32 [512, 12], P(('dp', 'fsdp'))
- grad_width_weight: float32 [512, 12], P(('dp', 'fsdp'))
All inputs are finite; a program needn't handle non-finite values. No bound on the sum of `fresh_flags` on one device may be relied on, other than what follows from the above.
Results may differ from a plain program's by a relative error of at most 0.014.
The roundings to bfloat16 on the way count: a program that leaves them out, or rounds other values in their place, can miss the bound.
Values may be sent and summed in bfloat16 or wider, within the bound.
A program may use at most 192 MiB of HBM per device.

v0:
```python
from functools import partial
import math

import jax
import jax.numpy as jnp
from jax import lax
from jax.sharding import PartitionSpec as P

epsilon = 1e-05
masked_score = -1e30


def layer_norm(values, scale_vec, shift_vec):
    centred = values - jnp.mean(values, axis=-1, keepdims=True)
    variance = jnp.mean(centred * centred, axis=-1, keepdims=True)
    return centred * lax.rsqrt(variance + epsilon) * scale_vec + shift_vec


def basis_tables(basis_count, sample_count):
    centers = (jnp.arange(basis_count, dtype=jnp.float32) + 0.5) / basis_count
    points = (jnp.arange(sample_count, dtype=jnp.float32) + 0.5) / sample_count
    offsets = (points[:, None] - centers[None, :]) * basis_count
    return (centers, jnp.exp(-0.5 * offsets * offsets))


def memory_weights(logits, mean_weight, width_weight, centers):
    basis_count = centers.shape[0]
    centre = jax.nn.sigmoid(jnp.sum(logits * mean_weight[:, None, :], axis=-1))
    variance = (jax.nn.softplus(jnp.sum(logits * width_weight[:, None, :], axis=-1)) + 0.5) * 0.02
    distance = centre[..., None] - centers
    return (
        1.0
        / basis_count
        * lax.rsqrt(variance)[..., None]
        * jnp.exp(-0.5 * distance * distance / variance[..., None])
    )


def causal_scores(queries, key_rows):
    length = queries.shape[0]
    factor = 1.0 / math.sqrt(queries.shape[-1])
    positions = jnp.arange(length)
    causal = positions[:, None] >= positions[None, :]
    scores = (
        jnp.einsum("qhe,khe->hqk", queries, key_rows, preferred_element_type=jnp.float32) * factor
    )
    return jnp.where(causal, scores, masked_score)


def attend_forward(seq_items, mean_weight, width_weight, centers):
    qkv_seq, mem_seq = seq_items
    queries = qkv_seq[:, 0]
    key_rows = qkv_seq[:, 1]
    value_rows = qkv_seq[:, 2]
    factor = 1.0 / math.sqrt(queries.shape[-1])
    scores = causal_scores(queries, key_rows)
    row_max = jnp.max(scores, axis=-1, keepdims=True)
    exponent = jnp.exp(scores - row_max)
    row_total = jnp.sum(exponent, axis=-1, keepdims=True)
    probs_low = (exponent / row_total).astype(jnp.bfloat16)
    log_total = row_max + jnp.log(row_total)
    logits = (
        jnp.einsum("qhe,jhe->hqj", queries, mem_seq[:, 0], preferred_element_type=jnp.float32)
        * factor
    )
    basis_low = memory_weights(logits, mean_weight, width_weight, centers).astype(jnp.bfloat16)
    attended = jnp.einsum("hqk,khe->qhe", probs_low, value_rows, preferred_element_type=jnp.float32)
    attended = attended + jnp.einsum(
        "hqj,jhe->qhe", basis_low, mem_seq[:, 1], preferred_element_type=jnp.float32
    )
    return (attended, log_total)


def attend_backward(seq_items, mean_weight, width_weight, centers):
    qkv_seq, mem_seq, log_total, grad_att = seq_items
    queries = qkv_seq[:, 0]
    key_rows = qkv_seq[:, 1]
    value_rows = qkv_seq[:, 2]
    mem_key = mem_seq[:, 0]
    mem_val = mem_seq[:, 1]
    factor = 1.0 / math.sqrt(queries.shape[-1])
    probs = jnp.exp(causal_scores(queries, key_rows) - log_total)
    probs_low = probs.astype(jnp.bfloat16)
    grad_values = jnp.einsum(
        "hqk,qhe->khe", probs_low, grad_att, preferred_element_type=jnp.float32
    )
    grad_probs = jnp.einsum(
        "qhe,khe->hqk", grad_att, value_rows, preferred_element_type=jnp.float32
    )
    inner = jnp.sum(grad_probs * probs, axis=-1, keepdims=True)
    grad_scores = (probs * (grad_probs - inner)).astype(jnp.bfloat16)
    grad_query = (
        jnp.einsum("hqk,khe->qhe", grad_scores, key_rows, preferred_element_type=jnp.float32)
        * factor
    )
    grad_keys = (
        jnp.einsum("hqk,qhe->khe", grad_scores, queries, preferred_element_type=jnp.float32)
        * factor
    )
    logits = (
        jnp.einsum("qhe,jhe->hqj", queries, mem_key, preferred_element_type=jnp.float32) * factor
    )
    basis, basis_back = jax.vjp(
        partial(memory_weights, centers=centers), logits, mean_weight, width_weight
    )
    basis_low = basis.astype(jnp.bfloat16)
    grad_mem_val = jnp.einsum(
        "hqj,qhe->jhe", basis_low, grad_att, preferred_element_type=jnp.float32
    )
    grad_basis = jnp.einsum("qhe,jhe->hqj", grad_att, mem_val, preferred_element_type=jnp.float32)
    grad_logits, grad_mean, grad_width = basis_back(grad_basis)
    logits_low = grad_logits.astype(jnp.bfloat16)
    grad_query = (
        grad_query
        + jnp.einsum("hqj,jhe->qhe", logits_low, mem_key, preferred_element_type=jnp.float32)
        * factor
    )
    grad_mem_key = (
        jnp.einsum("hqj,qhe->jhe", logits_low, queries, preferred_element_type=jnp.float32) * factor
    )
    grad_qkv = jnp.stack([grad_query, grad_keys, grad_values], axis=1).astype(jnp.bfloat16)
    grad_mem = jnp.stack([grad_mem_key, grad_mem_val], axis=1).astype(jnp.bfloat16)
    return (grad_qkv, grad_mem, grad_mean, grad_width)


def collect(
    gain_attn,
    shift_attn,
    qkv_weight,
    qv_bias,
    out_weight,
    out_bias,
    gain_mlp,
    shift_mlp,
    up_weight,
    up_bias,
    down_weight,
    down_bias,
    mean_weight,
    width_weight,
):
    return (
        lax.all_gather(gain_attn, ("dp", "fsdp"), axis=0, tiled=True),
        lax.all_gather(shift_attn, ("dp", "fsdp"), axis=0, tiled=True),
        lax.all_gather(qkv_weight, ("dp", "fsdp"), axis=0, tiled=True),
        lax.all_gather(qv_bias, ("dp", "fsdp"), axis=0, tiled=True),
        lax.all_gather(out_weight, ("dp", "fsdp"), axis=0, tiled=True),
        lax.all_gather(out_bias, ("dp", "fsdp"), axis=0, tiled=True),
        lax.all_gather(gain_mlp, ("dp", "fsdp"), axis=0, tiled=True),
        lax.all_gather(shift_mlp, ("dp", "fsdp"), axis=0, tiled=True),
        lax.all_gather(up_weight, ("dp", "fsdp"), axis=0, tiled=True),
        lax.all_gather(up_bias, ("dp", "fsdp"), axis=0, tiled=True),
        lax.all_gather(down_weight, ("dp", "fsdp"), axis=0, tiled=True),
        lax.all_gather(down_bias, ("dp", "fsdp"), axis=0, tiled=True),
        lax.all_gather(mean_weight, ("dp", "fsdp"), axis=0, tiled=True),
        lax.all_gather(width_weight, ("dp", "fsdp"), axis=0, tiled=True),
    )


def spread_grads(
    gain_attn,
    shift_attn,
    qkv_weight,
    qv_bias,
    out_weight,
    out_bias,
    gain_mlp,
    shift_mlp,
    up_weight,
    up_bias,
    down_weight,
    down_bias,
    mean_weight,
    width_weight,
):
    return (
        lax.psum_scatter(gain_attn, ("dp", "fsdp"), scatter_dimension=0, tiled=True),
        lax.psum_scatter(shift_attn, ("dp", "fsdp"), scatter_dimension=0, tiled=True),
        lax.psum_scatter(qkv_weight, ("dp", "fsdp"), scatter_dimension=0, tiled=True),
        lax.psum_scatter(qv_bias, ("dp", "fsdp"), scatter_dimension=0, tiled=True),
        lax.psum_scatter(out_weight, ("dp", "fsdp"), scatter_dimension=0, tiled=True),
        lax.psum_scatter(out_bias, ("dp", "fsdp"), scatter_dimension=0, tiled=True),
        lax.psum_scatter(gain_mlp, ("dp", "fsdp"), scatter_dimension=0, tiled=True),
        lax.psum_scatter(shift_mlp, ("dp", "fsdp"), scatter_dimension=0, tiled=True),
        lax.psum_scatter(up_weight, ("dp", "fsdp"), scatter_dimension=0, tiled=True),
        lax.psum_scatter(up_bias, ("dp", "fsdp"), scatter_dimension=0, tiled=True),
        lax.psum_scatter(down_weight, ("dp", "fsdp"), scatter_dimension=0, tiled=True),
        lax.psum_scatter(down_bias, ("dp", "fsdp"), scatter_dimension=0, tiled=True),
        lax.psum_scatter(mean_weight, ("dp", "fsdp"), scatter_dimension=0, tiled=True),
        lax.psum_scatter(width_weight, ("dp", "fsdp"), scatter_dimension=0, tiled=True),
    )


def shards(
    hidden,
    grad_out,
    past_states,
    old_coeffs,
    fresh_flags,
    ridge_map,
    gain_attn,
    shift_attn,
    qkv_weight,
    qv_bias,
    out_weight,
    out_bias,
    gain_mlp,
    shift_mlp,
    up_weight,
    up_bias,
    down_weight,
    down_bias,
    mean_weight,
    width_weight,
):
    seq_count, length, width_dim = hidden.shape
    token_count = seq_count * length
    heads = mean_weight.shape[1]
    head_dim = width_dim // heads
    basis_count = old_coeffs.shape[1]
    sample_count = ridge_map.shape[1] - length
    centers, sampled = basis_tables(basis_count, sample_count)
    keep_mask = (1 - fresh_flags).astype(jnp.bfloat16)
    old_kept = old_coeffs * keep_mask[:, None, None]
    old_signal = jnp.einsum(
        "ij,sjd->sid", sampled.astype(jnp.bfloat16), old_kept, preferred_element_type=jnp.float32
    ).astype(jnp.bfloat16)
    signal = jnp.concatenate([old_signal, past_states], axis=1)
    coeffs = jnp.einsum(
        "jt,std->sjd", ridge_map, signal, preferred_element_type=jnp.float32
    ).astype(jnp.bfloat16)
    gathered = collect(
        gain_attn,
        shift_attn,
        qkv_weight,
        qv_bias,
        out_weight,
        out_bias,
        gain_mlp,
        shift_mlp,
        up_weight,
        up_bias,
        down_weight,
        down_bias,
        mean_weight,
        width_weight,
    )
    (
        full_gain_attn,
        full_shift_attn,
        full_qkv,
        full_qv_bias,
        full_out,
        full_out_bias,
        full_gain_mlp,
        full_shift_mlp,
        full_up,
        full_up_bias,
        full_down,
        full_down_bias,
        full_mean,
        full_width,
    ) = gathered
    flat = hidden.reshape(token_count, width_dim).astype(jnp.float32)
    normed_low = layer_norm(
        flat, full_gain_attn.astype(jnp.float32), full_shift_attn.astype(jnp.float32)
    ).astype(jnp.bfloat16)
    bias_wide = full_qv_bias.astype(jnp.float32)
    bias_row = jnp.concatenate(
        [bias_wide[:width_dim], jnp.zeros((width_dim,), jnp.float32), bias_wide[width_dim:]]
    )
    qkv_low = (jnp.dot(normed_low, full_qkv, preferred_element_type=jnp.float32) + bias_row).astype(
        jnp.bfloat16
    )
    mem_low = jnp.einsum(
        "sjd,de->sje", coeffs, full_qkv[:, width_dim:], preferred_element_type=jnp.float32
    ).astype(jnp.bfloat16)
    qkv_seq = qkv_low.reshape(seq_count, length, 3, heads, head_dim)
    mem_seq = mem_low.reshape(seq_count, basis_count, 2, heads, head_dim)
    attended, log_total = lax.map(
        partial(
            attend_forward,
            mean_weight=full_mean.astype(jnp.float32).T,
            width_weight=full_width.astype(jnp.float32).T,
            centers=centers,
        ),
        (qkv_seq, mem_seq),
    )
    merged_low = attended.reshape(token_count, width_dim).astype(jnp.bfloat16)
    mid = (
        flat
        + jnp.dot(merged_low, full_out, preferred_element_type=jnp.float32)
        + full_out_bias.astype(jnp.float32)
    )
    normed_two = layer_norm(
        mid, full_gain_mlp.astype(jnp.float32), full_shift_mlp.astype(jnp.float32)
    ).astype(jnp.bfloat16)
    up_pre = jnp.dot(normed_two, full_up, preferred_element_type=jnp.float32) + full_up_bias.astype(
        jnp.float32
    )
    act_low = jax.nn.gelu(up_pre, approximate=True).astype(jnp.bfloat16)
    output = (
        mid
        + jnp.dot(act_low, full_down, preferred_element_type=jnp.float32)
        + full_down_bias.astype(jnp.float32)
    ).astype(jnp.bfloat16)
    weights_back = collect(
        gain_attn,
        shift_attn,
        qkv_weight,
        qv_bias,
        out_weight,
        out_bias,
        gain_mlp,
        shift_mlp,
        up_weight,
        up_bias,
        down_weight,
        down_bias,
        mean_weight,
        width_weight,
    )
    (
        back_gain_attn,
        back_shift_attn,
        back_qkv,
        back_qv_bias,
        back_out,
        back_out_bias,
        back_gain_mlp,
        back_shift_mlp,
        back_up,
        back_up_bias,
        back_down,
        back_down_bias,
        back_mean,
        back_width,
    ) = weights_back
    grad_low = grad_out.reshape(token_count, width_dim)
    grad_flat = grad_low.astype(jnp.float32)
    grad_down_weight = jnp.einsum(
        "tf,td->fd", act_low, grad_low, preferred_element_type=jnp.float32
    )
    grad_down_bias = jnp.sum(grad_flat, axis=0)
    grad_act = jnp.einsum("td,fd->tf", grad_low, back_down, preferred_element_type=jnp.float32)
    gelu_back = jax.vjp(partial(jax.nn.gelu, approximate=True), up_pre)[1]
    grad_up = gelu_back(grad_act)[0].astype(jnp.bfloat16)
    grad_up_weight = jnp.einsum(
        "td,tf->df", normed_two, grad_up, preferred_element_type=jnp.float32
    )
    grad_up_bias = jnp.sum(grad_up.astype(jnp.float32), axis=0)
    grad_normed_two = jnp.einsum("tf,df->td", grad_up, back_up, preferred_element_type=jnp.float32)
    norm_two_back = jax.vjp(
        layer_norm, mid, back_gain_mlp.astype(jnp.float32), back_shift_mlp.astype(jnp.float32)
    )[1]
    grad_mid_norm, grad_gain_mlp, grad_shift_mlp = norm_two_back(grad_normed_two)
    grad_mid = grad_flat + grad_mid_norm
    grad_proj = grad_mid.astype(jnp.bfloat16)
    grad_out_weight = jnp.einsum(
        "td,te->de", merged_low, grad_proj, preferred_element_type=jnp.float32
    )
    grad_out_bias = jnp.sum(grad_proj.astype(jnp.float32), axis=0)
    grad_merged = jnp.einsum(
        "te,de->td", grad_proj, back_out, preferred_element_type=jnp.float32
    ).astype(jnp.bfloat16)
    grad_qkv_seq, grad_mem_seq, grad_mean, grad_width = lax.map(
        partial(
            attend_backward,
            mean_weight=back_mean.astype(jnp.float32).T,
            width_weight=back_width.astype(jnp.float32).T,
            centers=centers,
        ),
        (qkv_seq, mem_seq, log_total, grad_merged.reshape(seq_count, length, heads, head_dim)),
    )
    grad_qkv = grad_qkv_seq.reshape(token_count, 3 * width_dim)
    grad_mem = grad_mem_seq.reshape(seq_count, basis_count, 2 * width_dim)
    grad_kv_weight = jnp.einsum("sjd,sje->de", coeffs, grad_mem, preferred_element_type=jnp.float32)
    grad_qkv_weight = jnp.einsum(
        "td,te->de", normed_low, grad_qkv, preferred_element_type=jnp.float32
    )
    grad_qkv_weight = grad_qkv_weight + jnp.concatenate(
        [jnp.zeros((width_dim, width_dim), jnp.float32), grad_kv_weight], axis=1
    )
    column_sums = jnp.sum(grad_qkv.astype(jnp.float32), axis=0)
    grad_qv_bias = jnp.concatenate([column_sums[:width_dim], column_sums[2 * width_dim :]])
    grad_normed = jnp.einsum("te,de->td", grad_qkv, back_qkv, preferred_element_type=jnp.float32)
    norm_one_back = jax.vjp(
        layer_norm, flat, back_gain_attn.astype(jnp.float32), back_shift_attn.astype(jnp.float32)
    )[1]
    grad_flat_norm, grad_gain_attn, grad_shift_attn = norm_one_back(grad_normed)
    grad_input = (grad_mid + grad_flat_norm).astype(jnp.bfloat16)
    grad_mean_rows = jnp.sum(grad_mean, axis=0).T
    grad_width_rows = jnp.sum(grad_width, axis=0).T
    summed = spread_grads(
        grad_gain_attn,
        grad_shift_attn,
        grad_qkv_weight,
        grad_qv_bias,
        grad_out_weight,
        grad_out_bias,
        grad_gain_mlp,
        grad_shift_mlp,
        grad_up_weight,
        grad_up_bias,
        grad_down_weight,
        grad_down_bias,
        grad_mean_rows,
        grad_width_rows,
    )
    return (
        output.reshape(seq_count, length, width_dim),
        grad_input.reshape(seq_count, length, width_dim),
        summed[0],
        summed[1],
        summed[2],
        summed[3],
        summed[4],
        summed[5],
        summed[6],
        summed[7],
        summed[8],
        summed[9],
        summed[10],
        summed[11],
        summed[12],
        summed[13],
    )


def solution(mesh):
    in_specs = (
        P(("dp", "fsdp"), None, None),
        P(("dp", "fsdp"), None, None),
        P(("dp", "fsdp"), None, None),
        P(("dp", "fsdp"), None, None),
        P(("dp", "fsdp")),
        P(),
        P(("dp", "fsdp")),
        P(("dp", "fsdp")),
        P(("dp", "fsdp"), None),
        P(("dp", "fsdp")),
        P(("dp", "fsdp"), None),
        P(("dp", "fsdp")),
        P(("dp", "fsdp")),
        P(("dp", "fsdp")),
        P(("dp", "fsdp"), None),
        P(("dp", "fsdp")),
        P(("dp", "fsdp"), None),
        P(("dp", "fsdp")),
        P(("dp", "fsdp"), None),
        P(("dp", "fsdp"), None),
    )
    out_specs = (
        P(("dp", "fsdp"), None, None),
        P(("dp", "fsdp"), None, None),
        P(("dp", "fsdp")),
        P(("dp", "fsdp")),
        P(("dp", "fsdp"), None),
        P(("dp", "fsdp")),
        P(("dp", "fsdp"), None),
        P(("dp", "fsdp")),
        P(("dp", "fsdp")),
        P(("dp", "fsdp")),
        P(("dp", "fsdp"), None),
        P(("dp", "fsdp")),
        P(("dp", "fsdp"), None),
        P(("dp", "fsdp")),
        P(("dp", "fsdp"), None),
        P(("dp", "fsdp"), None),
    )
    return jax.shard_map(shards, mesh=mesh, in_specs=in_specs, out_specs=out_specs, check_vma=False)
```

profile of v0, /device:TPU:0, one launch (start us, length us, event | category | flops | bytes accessed | tf_op | source)
XLA Modules:
  0.0 1203.7 jit_solution(3408999615956323460)
XLA Ops:
  15.8 42.9 %all-reduce.18 = (bf16[1536]{0:T(1024)(128)(2,1)S(1)}, bf16[768]{0:T(1024)(128)(2,1)S(1)}, bf16[768]{0:T(1024)(128)(2,1)S(1)}, bf16[768]{0:T(1024)(128)(2,1)S(1)...) all-reduce(bf16[1536]{0:T(1024)(128)(2,1)S(1)} %dynamic-update-slic, ...), channel_id=1, replica_groups=mesh['dp'=2,'fsdp'=16] {'dp','fsdp'}, use_global_device_ids=true, to_apply=%add.3 | all-reduce | flops 9216 | bytes 36864
  61.1 40.3 %all_gather.55 = bf16[512,12]{1,0:T(8,128)(2,1)S(1)} all-gather(bf16[16,12]{1,0:T(8,128)(2,1)S(1)} %copy-done.52), channel_id=1, replica_groups=mesh['dp'=2,'fsdp'=16] {'dp','fsdp'}, dimensions={0}, use_global_device_ids=true | all-gather | bytes 12672 | tf_op jit(solution)/shard_map/all_gather | solution.py:155
  101.5 37.2 %all_gather.54 = bf16[512,12]{1,0:T(8,128)(2,1)S(1)} all-gather(bf16[16,12]{1,0:T(8,128)(2,1)S(1)} %copy-done.53), channel_id=1, replica_groups=mesh['dp'=2,'fsdp'=16] {'dp','fsdp'}, dimensions={0}, use_global_device_ids=true | all-gather | bytes 12672 | tf_op jit(solution)/shard_map/all_gather | solution.py:156
  146.5 8.5 add_convert_fusion.11
  155.0 6.9 copy.96
  161.8 8.8 reshape.363
  170.7 5.8 copy.100
  176.5 4.1 convolution_convert_fusion
  180.6 4.7 copy.99
  185.3 56.6 %while.30 = (s32[]{:T(128)}, bf16[2,512,12,64]{1,3,2,0:T(8,128)(2,1)}, f32[2,12,512,1]{2,1,3,0:T(8,128)S(1)}, bf16[2,512,3,12,64]{1,4,3,2,0:T(8,128)(2,1)}, bf16...) while((s32[]{:T(128)}, ...), condition=%wide.region_7.8_spmd.clone, body=%wide.region_2.7_spmd.clone.sunk | while | flops 1680542720 | bytes 56774764 | solution.py:280
  191.7 5.8 fusion.193
  202.2 5.5 bitcast_dynamic-update-slice_fusion.7
  214.1 5.8 fusion.193
  224.6 5.5 bitcast_dynamic-update-slice_fusion.7
  246.6 3.4 fusion.150
  252.4 11.1 fusion.141
  263.5 15.5 %convert_reduce_fusion = (f32[3072]{0:T(1024)}, bf16[1024,3072]{1,0:T(8,128)(2,1)S(1)}) fusion(f32[1024,3072]{1,0:T(8,128)} %fusion.141, f32[3072]{0:T(1024)S(1)} %copy-done.49, bf16[1024,768]{1,0:T(8,128)(2,1)S(1)} %bitcast.289, bf16[3072,768]{1,0:T(8,128)(2,1)} %all-gather.11.cloned.1.call-done), kind=kOutput, calls=%fused_computation.150 | convolution fusion | flops 4904186880 | bytes 25190400 | tf_op jit(solution)/shard_map/td,fd->tf/dot_general | solution.py:345
  279.0 10.8 multiply_reduce_fusion.8
  302.6 118.5 %while.31 = (s32[]{:T(128)}, bf16[2,512,3,12,64]{1,4,3,2,0:T(8,128)(2,1)}, bf16[2,512,2,12,64]{1,4,3,2,0:T(8,128)(2,1)}, f32[2,12,512]{2,1,0:T(8,128)S(1)}, f32[...) while((s32[]{:T(128)}, ...), condition=%wide.region_21.22_spmd.clone, body=%wide.region_12.21_spmd.clone.sunk | while | flops 4210654208 | bytes 268434000 | solution.py:366
  308.7 4.0 fusion.202
  312.7 5.9 multiply_reduce_fusion.17
  318.7 10.3 fusion.205
  331.2 3.7 fusion.207
  338.4 7.1 multiply_reduce_fusion.16
  345.4 7.0 multiply_convert_fusion.16
  355.7 3.7 fusion.206
  367.7 4.0 fusion.202
  371.7 5.9 multiply_reduce_fusion.17
  377.6 10.3 fusion.205
  390.2 3.7 fusion.207
  397.4 7.1 multiply_reduce_fusion.16
  404.4 7.0 multiply_convert_fusion.16
  414.6 3.7 fusion.206
  423.1 4.8 fusion.151
  429.7 9.4 copy.109
  439.1 4.1 copy.128
  445.9 6.3 pad_add_fusion
  452.9 11.0 fusion.140
  464.6 13.4 %fusion.142 = f32[3072,768]{1,0:T(8,128)} fusion(bf16[1024,768]{1,0:T(8,128)(2,1)} %bitcast.288, f32[1024,3072]{1,0:T(8,128)} %fusion.141, f32[3072]{0:T(1024)S(1)} %copy-done.50), kind=kOutput, calls=%fused_computation.237 | convolution fusion | flops 4863295488 | bytes 23605248 | tf_op jit(solution)/shard_map/tf,td->fd/dot_general | solution.py:341
  483.6 7.5 fusion.143
  494.5 39.4 %all-reduce.17 = (f32[768]{0:T(1024)S(1)}, f32[768]{0:T(1024)S(1)}, f32[1536]{0:T(1024)S(1)}, f32[768]{0:T(1024)S(1)}, f32[768]{0:T(1024)S(1)}, /*index=5*/f32[7...) all-reduce(f32[768]{0:T(1024)S(1)} %get-tuple-element.285, ...), channel_id=2, replica_groups=mesh['dp'=2,'fsdp'=16] {'dp','fsdp'}, use_global_device_ids=true, to_apply=%region_25.26.clone | all-reduce | flops 9216 | bytes 73728
  538.6 5.1 add_convert_fusion.12
  543.7 13.1 %add_convert_fusion.13 = bf16[1024,768]{1,0:T(8,128)(2,1)} fusion(f32[1024,768]{1,0:T(8,128)S(1)} %copy-done.7, bf16[3072,768]{1,0:T(8,128)(2,1)} %all-gather.11.cloned.1.call-done, f32[768]{0:T(1024)S(1)} %convert_element_type.173, f32[1024,3072]{1,0:T(8,128)} %fusion.141, f32[3072]{0:T(1024)S(1)} %copy-done.50), kind=kOutput, calls=%fused_computation.189 | convolution fusion | flops 4865654784 | bytes 22035456 | tf_op jit(solution)/shard_map/dot_general | solution.py:304
  556.8 129.9 %reduce-scatter.19.cloned.1.call-done = f32[16,12]{1,0:T(8,128)} async-done(((f32[512,12]{1,0:T(8,128)}), f32[16,12]{1,0:T(8,128)}) %reduce-scatter.19.cloned.1.call-update) | async-done | bytes 784
  686.7 101.2 %reduce-scatter.13.cloned.1.call-done = f32[24,768]{1,0:T(8,128)} async-done(((f32[768,768]{1,0:T(8,128)}), f32[24,768]{1,0:T(8,128)}) %reduce-scatter.13.cloned.1.call-update) | async-done | bytes 73744 | tf_op jit(solution)/shard_map/reduce_scatter | solution.py:181
  787.9 125.4 %reduce-scatter.11.cloned.1.call-done = f32[24,2304]{1,0:T(8,128)} async-done(((f32[768,2304]{1,0:T(8,128)}), f32[24,2304]{1,0:T(8,128)}) %reduce-scatter.11.cloned.1.call-update) | async-done | bytes 221200 | tf_op jit(solution)/shard_map/reduce_scatter | solution.py:179
  913.2 141.4 %reduce-scatter.15.cloned.1.call-done = f32[24,3072]{1,0:T(8,128)} async-done(((f32[768,3072]{1,0:T(8,128)}), f32[24,3072]{1,0:T(8,128)}) %reduce-scatter.15.cloned.1.call-update) | async-done | bytes 294928 | tf_op jit(solution)/shard_map/reduce_scatter | solution.py:185
  1054.6 141.8 %reduce-scatter.17.cloned.1.call-done = f32[96,768]{1,0:T(8,128)} async-done(((f32[3072,768]{1,0:T(8,128)}), f32[96,768]{1,0:T(8,128)}) %reduce-scatter.17.cloned.1.call-update) | async-done | bytes 294928 | tf_op jit(solution)/shard_map/reduce_scatter | solution.py:187
  (361 shorter events, 115.7 us)
Async XLA Ops:
  7.2 134.4 %copy-start = (bf16[512,1024]{1,0:T(8,128)(2,1)S(1)}, bf16[512,1024]{1,0:T(8,128)(2,1)}, u32[]{:S(2)}) copy-start(bf16[512,1024]{1,0:T(8,128)(2,1)} %param.29) | copy-start | bytes 3145732
  7.2 6.7 copy-start.64
  7.2 6.9 copy-start.65
  7.2 7.1 copy-start.66
  7.2 7.4 copy-start.67
  7.3 7.6 copy-start.68
  7.3 7.8 copy-start.69
  7.3 8.0 copy-start.70
  7.3 8.3 copy-start.71
  7.3 53.8 %copy-start.52 = (bf16[16,12]{1,0:T(8,128)(2,1)S(1)}, bf16[16,12]{1,0:T(8,128)(2,1)}, u32[]{:S(2)}) copy-start(bf16[16,12]{1,0:T(8,128)(2,1)} %param.42) | copy-start | bytes 1156
  7.3 94.2 %copy-start.53 = (bf16[16,12]{1,0:T(8,128)(2,1)S(1)}, bf16[16,12]{1,0:T(8,128)(2,1)}, u32[]{:S(2)}) copy-start(bf16[16,12]{1,0:T(8,128)(2,1)} %param.43) | copy-start | bytes 1156
  7.3 139.1 %all-gather.5.cloned.1.call-start = ((), (), s32[]{:S(2)}) async-start(), calls=%async_computation.6 | async-start | bytes 3649536 | tf_op jit(solution)/shard_map/all_gather | solution.py:145
  8.0 238.6 %all-gather.7.cloned.1.call-start = ((), (), s32[]{:S(2)}) async-start(), calls=%async_computation.7 | async-start | bytes 1216512 | tf_op jit(solution)/shard_map/all_gather | solution.py:147
  8.8 243.5 %all-gather.9.cloned.1.call-start = ((), (), s32[]{:S(2)}) async-start(), calls=%async_computation.8 | async-start | bytes 4866048 | tf_op jit(solution)/shard_map/all_gather | solution.py:151
  9.5 254.0 %all-gather.11.cloned.1.call-start = ((), (), s32[]{:S(2)}) async-start(), calls=%async_computation.9 | async-start | bytes 4866048 | tf_op jit(solution)/shard_map/all_gather | solution.py:153
  10.1 546.7 %reduce-scatter.21.cloned.1.call-start = ((), (), s32[]{:S(2)}) async-start(), calls=%async_computation.15 | async-start | bytes 270336
  12.6 132.0 %copy-start.27 = (f32[1,4,2,128]{3,1,2,0:T(4,128)}, f32[1,4,2,128]{3,1,2,0:T(4,128)S(1)}, u32[]{:S(2)}) copy-start(f32[1,4,2,128]{3,1,2,0:T(4,128)S(1)} %copy.125) | copy-start | bytes 12292
  13.9 45.4 %copy-start.45 = (f32[1,4,2,128]{3,1,2,0:T(4,128)}, f32[1,4,2,128]{3,1,2,0:T(4,128)S(1)}, u32[]{:S(2)}) copy-start(f32[1,4,2,128]{3,1,2,0:T(4,128)S(1)} %copy.126) | copy-start | bytes 12292
  13.9 130.8 %copy-start.29 = (f32[1024]{0:T(1024)}, f32[1024]{0:T(1024)S(1)}, u32[]{:S(2)}) copy-start(f32[1024]{0:T(1024)S(1)} %rsqrt.39) | copy-start | bytes 12292
  58.7 86.0 %copy-start.23 = (f32[768]{0:T(1024)}, f32[768]{0:T(1024)S(1)}, u32[]{:S(2)}) copy-start(f32[768]{0:T(1024)S(1)} %convert_element_type.153) | copy-start | bytes 9220
  59.3 85.4 %copy-start.41 = (f32[768]{0:T(1024)}, f32[768]{0:T(1024)S(1)}, u32[]{:S(2)}) copy-start(f32[768]{0:T(1024)S(1)} %convert_element_type.154) | copy-start | bytes 9220
  170.7 5.8 copy-start.58
  170.7 5.8 copy-start.72
  250.1 39.8 %copy-start.19 = (f32[1024]{0:T(1024)}, f32[1024]{0:T(1024)S(1)}, u32[]{:S(2)}) copy-start(f32[1024]{0:T(1024)S(1)} %broadcast_multiply_fusion.6) | copy-start | bytes 12292
  252.3 37.6 %copy-start.21 = (f32[1024]{0:T(1024)}, f32[1024]{0:T(1024)S(1)}, u32[]{:S(2)}) copy-start(f32[1024]{0:T(1024)S(1)} %fusion.132) | copy-start | bytes 12292
  252.3 11.2 copy-start.13
  252.3 11.2 copy-start.49
  263.5 15.5 %copy-start.6 = (f32[1024,768]{1,0:T(8,128)S(1)}, f32[1024,768]{1,0:T(8,128)}, u32[]{:S(2)}) copy-start(f32[1024,768]{1,0:T(8,128)} %copy-done.5) | copy-start | bytes 9437188
  279.0 10.9 copy-start.15
  303.0 35.4 %copy-start.10 = (bf16[2,512,12,64]{1,3,2,0:T(8,128)(2,1)}, bf16[2,512,12,64]{1,3,2,0:T(8,128)(2,1)S(1)}, u32[]{:S(2)}) copy-start(bf16[2,512,12,64]{1,3,2,0:T(8,128)(2,1)S(1)} %get-tuple-element.597) | copy-start | bytes 4718596 | tf_op jit(solution)/shard_map/while
  318.6 10.4 slice-start
  318.6 10.4 slice-start.1
  318.7 10.4 slice-start.2
  338.4 7.1 copy-start.60
  362.0 35.4 %copy-start.10 = (bf16[2,512,12,64]{1,3,2,0:T(8,128)(2,1)}, bf16[2,512,12,64]{1,3,2,0:T(8,128)(2,1)S(1)}, u32[]{:S(2)}) copy-start(bf16[2,512,12,64]{1,3,2,0:T(8,128)(2,1)S(1)} %get-tuple-element.597) | copy-start | bytes 4718596 | tf_op jit(solution)/shard_map/while
  377.6 10.4 slice-start
  377.6 10.4 slice-start.1
  377.6 10.4 slice-start.2
  397.3 7.1 copy-start.60
  422.0 264.7 %reduce-scatter.19.cloned.1.call-start = ((), (), s32[]{:S(2)}) async-start(), calls=%async_computation.14 | async-start | bytes 270336
  423.0 364.9 %reduce-scatter.13.cloned.1.call-start = ((), (), s32[]{:S(2)}) async-start(), calls=%async_computation.11 | async-start | bytes 2433024 | tf_op jit(solution)/shard_map/reduce_scatter | solution.py:181
  427.9 485.4 %reduce-scatter.11.cloned.1.call-start = ((), (), s32[]{:S(2)}) async-start(), calls=%async_computation.10 | async-start | bytes 7299072 | tf_op jit(solution)/shard_map/reduce_scatter | solution.py:179
  452.2 602.4 %reduce-scatter.15.cloned.1.call-start = ((), (), s32[]{:S(2)}) async-start(), calls=%async_computation.12 | async-start | bytes 9732096 | tf_op jit(solution)/shard_map/reduce_scatter | solution.py:185
  463.9 732.5 %reduce-scatter.17.cloned.1.call-start = ((), (), s32[]{:S(2)}) async-start(), calls=%async_computation.13 | async-start | bytes 9732096 | tf_op jit(solution)/shard_map/reduce_scatter | solution.py:187
  483.5 7.6 copy-start.46
  483.6 9.2 copy-start.30
  491.1 47.5 %copy-start.44 = (f32[1024]{0:T(1024)S(1)}, f32[1024]{0:T(1024)}, u32[]{:S(2)}) copy-start(f32[1024]{0:T(1024)} %copy-done.43) | copy-start | bytes 12292
  543.7 652.7 %copy-start.1 = (bf16[512,1024]{1,0:T(8,128)(2,1)S(1)}, bf16[512,1024]{1,0:T(8,128)(2,1)}, u32[]{:S(2)}) copy-start(bf16[512,1024]{1,0:T(8,128)(2,1)} %param.29) | copy-start | bytes 3145732
  (56 other events, 174.0 us)
Sparse Core Ops, SparseCore 0:
  11.0 62.8 all-gather.4
  76.8 52.7 all-gather.6
  132.5 62.5 all-gather.8
  197.9 62.3 all-gather.10
  422.1 131.9 reduce-scatter.20
  556.9 129.7 reduce-scatter.18
  692.5 95.3 reduce-scatter.12
  795.1 118.1 reduce-scatter.10
  919.7 134.8 reduce-scatter.14
  1061.9 134.4 reduce-scatter.16
where the time goes:
time: 1210 us; the launch traced here: 1200 us
  waiting for transfers between devices  642 us (53%)
  matrix products  239 us (20%)
  blocking collectives  160 us (13%)
  local copies, waits for them, and re-layouts  84.7 us (7%)
  other arithmetic  49.3 us (4%)
  between operations  15.5 us (1%)
  loops' own time  13.2 us (1%)
    reduce_scatter x1, waiting for transfers between devices, spread_grads(): lax.psum_scatter(down_weight, ('dp', 'fsdp'), scatter_dimension=0, tiled=...  142 us
    reduce_scatter x1, waiting for transfers between devices, spread_grads(): lax.psum_scatter(up_weight, ('dp', 'fsdp'), scatter_dimension=0, tiled=True)  141 us
    unnamed x12, waiting for transfers between devices  133 us
    reduce_scatter x1, waiting for transfers between devices, spread_grads(): lax.psum_scatter(qkv_weight, ('dp', 'fsdp'), scatter_dimension=0, tiled=T...  125 us
    reduce_scatter x1, waiting for transfers between devices, spread_grads(): lax.psum_scatter(out_weight, ('dp', 'fsdp'), scatter_dimension=0, tiled=T...  101 us
    unnamed x2, blocking collectives  82.3 us
    all_gather x1, blocking collectives, collect(): lax.all_gather(mean_weight, ('dp', 'fsdp'), axis=0, tiled=True)  40.3 us
    all_gather x1, blocking collectives, collect(): lax.all_gather(width_weight, ('dp', 'fsdp'), axis=0, tiled=True)  37.2 us
  transfers between devices with their start and end apart: 10, of which 5 were waited for; matrix products, arithmetic and copies ran while one was open for 17% of the time, Pallas kernels for 0%

commit v1 on v0

v1 whole, which is shorter than its diff:
```python
import math

import jax
import jax.numpy as jnp
from jax import lax
from jax.experimental import pallas as pl
from jax.experimental.pallas import tpu as pltpu
from jax.sharding import PartitionSpec as P

EPS = 1e-05
LOG2E = 1.4426950408889634
BF = jnp.bfloat16
F32 = jnp.float32
AXES = ("dp", "fsdp")
VMEM_BYTES = 60 * 1024 * 1024


def dot_nn(a, b):
    return lax.dot_general(a, b, (((1,), (0,)), ((), ())), preferred_element_type=F32)


def dot_nt(a, b):
    return lax.dot_general(a, b, (((1,), (1,)), ((), ())), preferred_element_type=F32)


def dot_tn(a, b):
    return lax.dot_general(a, b, (((0,), (0,)), ((), ())), preferred_element_type=F32)


def split_high_low(x):
    high = x.astype(BF)
    return high, (x - high.astype(F32)).astype(BF)


def iota(shape, dim):
    return lax.broadcasted_iota(jnp.int32, shape, dim)


def head_masks(pair_lanes, head_dim):
    lane = iota((1, pair_lanes), 1)
    return [((lane // head_dim) == h).astype(F32).astype(BF) for h in range(pair_lanes // head_dim)]


def norm_parts(x):
    mean = jnp.mean(x, axis=-1, keepdims=True)
    centred = x - mean
    variance = jnp.mean(centred * centred, axis=-1, keepdims=True)
    inv = lax.rsqrt(variance + EPS)
    return centred * inv, inv


def norm_back(grad, unit, inv, gain):
    g = grad * gain
    return inv * (g - jnp.mean(g, axis=-1, keepdims=True) - unit * jnp.mean(g * unit, axis=-1, keepdims=True))


MESH = pl.DeviceIdType.MESH


class Place:
    def __init__(self):
        self.y = lax.axis_index("dp")
        f = lax.axis_index("fsdp")
        self.z, self.x, self.c = f // 4, (f // 2) % 2, f % 2

    def at(self, y=None, z=None, x=None, c=None):
        y, z, x, c = (b if a is None else a for a, b in ((y, self.y), (z, self.z), (x, self.x), (c, self.c)))
        return (y, z * 4 + x * 2 + c)

    def far_z(self, s):
        return (self.z + s) % 4

    def others(self):
        return [self.at(c=1 - self.c), self.at(x=1 - self.x), self.at(y=1 - self.y)] + [
            self.at(z=self.far_z(s)) for s in (1, 2, 3)]

    def layer(self):
        return [self.at(y=(self.y + d // 4) % 2, x=(self.x + d // 2) % 2, c=(self.c + d) % 2) for d in range(1, 8)] + [
            self.at(z=self.far_z(s)) for s in (1, 2, 3)]

    def greet(self, devices):
        barrier = pltpu.get_barrier_semaphore()
        for d in devices:
            pl.semaphore_signal(barrier, inc=1, device_id=d, device_id_type=MESH)
        pl.semaphore_wait(barrier, len(devices))


class Weight:
    def __init__(self, index, rows, half, parts):
        self.index, self.rows, self.half, self.parts = index, rows, half, parts

    def where(self, part, c=None):
        r0, rn, c0, cn = self.parts[part]
        if c is None:
            return pl.ds(r0, rn), pl.ds(c0, cn)
        return pl.ds(r0, rn), pl.ds(pl.multiple_of(c * self.half + c0, 128), cn)

    def columns(self, c):
        return pl.ds(pl.multiple_of(c * self.half, 128), self.half)


def split_columns(n):
    first = (n // 128 + 1) // 2 * 128
    return first


def weight_table(width, ff, devices):
    chip = 2 * width // devices
    chip_ff = 2 * ff // devices
    items = []
    for i, n in enumerate((3 * width, width, ff)):
        half = n // 2
        first = split_columns(half)
        items.append(Weight(i, chip, half, ((0, chip, 0, first), (0, chip, first, half - first))))
    half = width // 2
    items.append(Weight(3, chip_ff, half, ((0, chip_ff // 2, 0, half), (chip_ff // 2, chip_ff // 2, 0, half))))
    return items


def nested(conds, act):
    if not conds:
        act()
        return

    @pl.when(conds[0]())
    def _():
        nested(conds[1:], act)


class Started:
    def __init__(self, send, recv):
        self.send, self.recv, self.live = send, recv, {}

    def go(self, name, src, dst, slot, dev):
        copy = pltpu.make_async_remote_copy(
            src_ref=src, dst_ref=dst, send_sem=self.send.at[slot], recv_sem=self.recv.at[slot],
            device_id=dev, device_id_type=MESH)
        copy.start()
        self.live.setdefault(name, []).append(copy)

    def arrived(self, name):
        for copy in self.live[name]:
            copy.wait_recv()

    def left(self, name=None):
        for key in list(self.live) if name is None else [name]:
            for copy in self.live.pop(key):
                copy.wait_send()


class Gather:
    SLOTS = 2 * 23

    def __init__(self, place, send, recv, base, w, full):
        self.p, self.send, self.recv, self.base, self.w, self.full = place, send, recv, base, w, full
        self.begun = []

    def ref(self, part, y, z, x):
        if part is None:
            return self.full.at[y, z, x, :, self.w.columns(self.p.c)]
        r, c = self.w.where(part, self.p.c)
        return self.full.at[y, z, x, r, c]

    def go(self, src, dst, send, recv, dev, conds, like):
        pltpu.make_async_remote_copy(
            src_ref=src, dst_ref=dst, send_sem=self.send.at[self.base + send()], recv_sem=self.recv.at[self.base + recv],
            device_id=dev, device_id_type=MESH).start()
        self.begun.append((send, conds, like))

    def wait(self, ref, slot):
        pltpu.make_async_remote_copy(
            src_ref=ref, dst_ref=ref, send_sem=self.send.at[self.base], recv_sem=self.recv.at[self.base + slot],
            device_id=self.p.at(c=1 - self.p.c), device_id_type=MESH).wait_recv()

    def left(self):
        for send, conds, like in self.begun:
            def act():
                pltpu.make_async_remote_copy(
                    src_ref=like(), dst_ref=like(), send_sem=self.send.at[self.base + send()], recv_sem=self.recv.at[self.base],
                    device_id=self.p.at(c=1 - self.p.c), device_id_type=MESH).wait_send()

            nested(conds, act)

    def along(self, j, act):
        here = self.p.z
        for z, cond, toward in ((lambda: here - j, lambda: here >= j, 1), (lambda: here + j, lambda: here + j <= 3, -1)):
            nested((cond,), lambda: act(z, (cond,), toward))

    def pass_z(self, src, dst, z, toward, conds, like):
        p = self.p
        more = (lambda: p.z <= 2) if toward == 1 else (lambda: p.z >= 1)
        nested((more,), lambda: self.go(
            src, dst, lambda: z() + (0 if toward == 1 else 4), z(), p.at(z=p.z + toward), conds + (more,), like))

    def partner(self, part, step):
        p = self.p
        return p.at(x=1 - p.x) if (part + step) % 2 == 0 else p.at(y=1 - p.y)

    def behind(self, part):
        p = self.p
        return (p.y, 1 - p.x) if part == 0 else (1 - p.y, p.x)

    def own_z(self):
        return self.p.z

    def one(self, part):
        return self.ref(part, 0, 0, 0)

    def start(self, block):
        p = self.p
        for toward in (1, -1):
            self.pass_z(block, self.ref(None, p.y, p.z, p.x), self.own_z, toward, (), lambda: self.one(None))
        for part in (0, 1):
            self.onward(part, self.own_z, block.at[self.w.where(part)], ())

    def onward(self, part, z, src, conds):
        p = self.p
        dst = self.ref(part, p.y, z(), p.x)
        o = part * 23
        like = lambda: self.one(part)
        self.go(src, dst, lambda: o + 8 + z(), o + 8 + z(), self.partner(part, 0), conds, like)
        self.go(src, dst, lambda: o + 12 + z(), o + 12 + z(), self.partner(part, 1), conds, like)

    def on_z(self, j):
        def act(z, conds, toward):
            whole = self.ref(None, self.p.y, z(), self.p.x)
            self.wait(whole, z())
            self.pass_z(whole, whole, z, toward, conds, lambda: self.one(None))
            for part in (0, 1):
                self.onward(part, z, self.ref(part, self.p.y, z(), self.p.x), conds)

        self.along(j, act)

    def on_second(self, j):
        def act(z, conds, toward):
            for part in (0, 1):
                self.second_on(part, z, conds)

        if j == 0:
            act(self.own_z, (), 0)
        else:
            self.along(j, act)

    def second_on(self, part, z, conds):
        y, x = self.behind(part)
        ref = self.ref(part, y, z(), x)
        o = part * 23
        self.wait(ref, o + 8 + z())
        self.go(ref, ref, lambda: o + 16 + z(), o + 16 + z(), self.partner(part, 1), conds, lambda: self.one(part))

    def core(self, step):
        p = self.p
        for part in (0, 1):
            o = part * 23
            if step == 2:
                for z in range(4):
                    y, x = (1 - p.y, p.x) if part == 0 else (p.y, 1 - p.x)
                    self.wait(self.ref(part, y, z, x), o + 12 + z)
                    self.wait(self.ref(part, 1 - p.y, z, 1 - p.x), o + 16 + z)
            self.go_core(lambda part=part: self.of_step(part, step), o + 20 + step)

    def of_step(self, part, step):
        p = self.p
        if step == 0:
            y, x = p.y, p.x
        elif step == 1:
            y, x = self.behind(part)
        else:
            y, x = (1 - p.y, slice(None)) if part == 0 else (slice(None), 1 - p.x)
        return self.ref(part, y, slice(None), x)

    def go_core(self, make, slot):
        self.go(make(), make(), lambda: slot, slot, self.p.at(c=1 - self.p.c), (), make)

    def finish(self):
        p = self.p
        for part in (0, 1):
            r, c = self.w.where(part, 1 - p.c)
            for step in range(3):
                if step == 2:
                    ref = self.full.at[1 - p.y, :, :, r, c] if part == 0 else self.full.at[:, :, 1 - p.x, r, c]
                else:
                    y, x = (p.y, p.x) if step == 0 else self.behind(part)
                    ref = self.full.at[y, :, x, r, c]
                self.wait(ref, part * 23 + 20 + step)


class LateGather(Gather):
    def start(self, block):
        for part in (0, 1):
            self.onward(part, self.own_z, block.at[self.w.where(part)], ())

    def on_third(self):
        p = self.p
        for part in (0, 1):
            o = part * 23
            y, x = (1 - p.y, p.x) if part == 0 else (p.y, 1 - p.x)
            self.wait(self.ref(part, y, p.z, x), o + 12 + p.z)
            self.wait(self.ref(part, 1 - p.y, p.z, 1 - p.x), o + 16 + p.z)
        ref = self.layer(p.z)
        for toward in (1, -1):
            self.pass_z(ref, ref, self.own_z, toward, (), lambda: self.layer(0))

    def layer(self, z):
        return self.ref(None, slice(None), z, slice(None))

    def on_z(self, j):
        def act(z, conds, toward):
            ref = self.layer(z())
            self.wait(ref, z())
            self.pass_z(ref, ref, z, toward, conds, lambda: self.layer(0))

        self.along(j, act)

    def core(self):
        self.go_core(lambda: self.ref(None, slice(None), slice(None), slice(None)), 20)

    def finish(self):
        self.wait(self.full.at[:, :, :, :, self.w.columns(1 - self.p.c)], 20)


def middle_body(
    att, hidden, gout, wout, wup, wdown, vecs, ubias, vsum, usum,
    x_t, dout, mid, x, acc, gacc, act_s, slope_s, outs, local, sem, put_down, put_up, hook,
):
    output_h, gmid_h, gatt_h, dout_h = outs
    tokens, width = hidden.shape
    ff = wup.shape[1]
    block = 256
    blocks = tokens // block
    chunk = ubias.shape[1]
    chunks = ff // chunk
    out_bias, gain, shift, down_bias = (vecs[i:i + 1, :] for i in (4, 5, 6, 7))

    def enter(i, _):
        r = pl.ds(pl.multiple_of(i * block, block), block)
        m = hidden[r, :].astype(F32) + dot_nn(att[r, :], wout[...]) + out_bias
        mid[r, :] = m
        unit, _ = norm_parts(m)
        y = (unit * gain + shift).astype(BF)
        x[r, :] = y
        x_t[:, r] = y.T
        acc[r, :] = jnp.zeros((block, width), F32)
        gacc[r, :] = jnp.zeros((block, width), F32)
        hook("enter", i)
        return 0

    lax.fori_loop(0, blocks, enter, 0)
    hook("entered", 0)

    def chunk_of(i):
        return (i % 2) * 2 + i // 2

    def first(i):
        j = chunk_of(i)
        c = pl.ds(pl.multiple_of(j * chunk, chunk), chunk)
        slot = i % 2
        w_up = wup[:, c]
        bias = ubias[pl.ds(j, 1), :]
        for b in range(blocks):
            r = slice(b * block, (b + 1) * block)
            u = dot_nn(x[r, :], w_up) + bias
            u2 = u * u
            th = jnp.tanh(u * (0.7978845608028654 + 0.7978845608028654 * 0.044715 * u2))
            half_one = 0.5 + 0.5 * th
            act_s[slot, r, :] = (u * half_one).astype(BF)
            slope = half_one + (0.5 * u) * (1.0 - th * th) * (
                0.7978845608028654 + 3 * 0.7978845608028654 * 0.044715 * u2)
            slope_s[slot, r, :] = slope.astype(BF)
        for k in range(2):
            part = slice(k * chunk // 2, (k + 1) * chunk // 2)
            put_down(i, k, dot_tn(act_s[slot, :, part], gout[...]).astype(BF))
        hook("first", i)

    def second(i):
        j = chunk_of(i)
        c = pl.ds(pl.multiple_of(j * chunk, chunk), chunk)
        slot = i % 2
        w_up, w_down = wup[:, c], wdown[c, :]
        colsum = jnp.zeros((1, chunk), F32)
        for b in range(blocks):
            r = slice(b * block, (b + 1) * block)
            gu = (dot_nt(gout[r, :], w_down) * slope_s[slot, r, :].astype(F32)).astype(BF)
            colsum = colsum + jnp.sum(gu.astype(F32), axis=0, keepdims=True)
            slope_s[slot, r, :] = gu
            acc[r, :] += dot_nn(act_s[slot, r, :], w_down)
            gacc[r, :] += dot_nt(gu, w_up)
        usum[pl.ds(j, 1), :] = colsum
        hook("middle", i)
        for k in range(2):
            part = slice(k * width // 2, (k + 1) * width // 2)
            put_up(i, k, dot_nn(x_t[part, :], slope_s[slot]).astype(BF))
        hook("second", i)

    def ahead(i, _):
        first(i)
        return 0

    lax.fori_loop(0, 2, ahead, 0)
    hook("ready", 0)
    usum[...] = jnp.zeros_like(usum)

    def both(i, _):
        second(i)

        @pl.when(i + 2 < chunks)
        def _():
            first(i + 2)

        hook("both", i)
        return 0

    lax.fori_loop(0, chunks, both, 0)
    vsum[...] = jnp.zeros_like(vsum)

    def rows_out(i):
        r = pl.ds(pl.multiple_of(i * block, block), block)
        return (pltpu.make_async_copy(act_s.at[0, r, :], output_h.at[r, :], local.at[sem + 1 + 3 * i]),
                pltpu.make_async_copy(mid.at[r, :], gmid_h.at[r, :], local.at[sem + 2 + 3 * i]),
                pltpu.make_async_copy(act_s.at[1, r, :], gatt_h.at[r, :], local.at[sem + 3 + 3 * i]))

    def leave(i, _):
        r = pl.ds(pl.multiple_of(i * block, block), block)
        m = mid[r, :]
        act_s[0, r, :] = (m + acc[r, :] + down_bias).astype(BF)
        unit, inv = norm_parts(m)
        g = gacc[r, :]
        go = gout[r, :].astype(F32)
        gm = go + norm_back(g, unit, inv, gain)
        mid[r, :] = gm
        gp = gm.astype(BF)
        x[r, :] = gp
        act_s[1, r, :] = dot_nt(gp, wout[...]).astype(BF)
        for copy in rows_out(i):
            copy.start()
        vsum[0:1, :] += jnp.sum(go, axis=0, keepdims=True)
        vsum[1:2, :] += jnp.sum(g * unit, axis=0, keepdims=True)
        vsum[2:3, :] += jnp.sum(g, axis=0, keepdims=True)
        vsum[3:4, :] += jnp.sum(gp.astype(F32), axis=0, keepdims=True)
        hook("leave", i)
        return 0

    lax.fori_loop(0, blocks, leave, 0)
    for j in range(width // 256):
        c = slice(j * 256, (j + 1) * 256)
        dout[:, c] = dot_tn(att[...], x[:, c]).astype(BF)
    final = pltpu.make_async_copy(dout, dout_h, local.at[sem])
    final.start()
    hook("end", 0)
    for i in range(blocks):
        for copy in rows_out(i):
            copy.wait()
    final.wait()


def middle_scratch(tokens, width, chunk):
    return [
        pltpu.VMEM((tokens, width), F32),
        pltpu.VMEM((tokens, width), BF),
        pltpu.VMEM((tokens, width), F32),
        pltpu.VMEM((tokens, width), F32),
        pltpu.VMEM((2, tokens, chunk), BF),
        pltpu.VMEM((2, tokens, chunk), BF),
    ]


def middle_call(att, hidden, gout, wout, wup, wdown, vecs, ubias):
    tokens, width = att.shape
    ff = wup.shape[1]
    chunk = ubias.shape[1]
    vm = pl.BlockSpec(memory_space=pltpu.VMEM)
    anyw = pl.BlockSpec(memory_space=pl.ANY)
    shapes = (
        jax.ShapeDtypeStruct((tokens, width), BF),
        jax.ShapeDtypeStruct((tokens, width), F32),
        jax.ShapeDtypeStruct((tokens, width), BF),
        jax.ShapeDtypeStruct((width, width), BF),
        jax.ShapeDtypeStruct((width, ff), BF),
        jax.ShapeDtypeStruct((ff, width), BF),
        jax.ShapeDtypeStruct((8, width), F32),
        jax.ShapeDtypeStruct((8, chunk), F32),
    )

    def kernel(att, hidden, gout, wout, wup, wdown, vecs, ubias, o, gm, ga, do, du, dd, vsum, usum, *scratch):
        def place(i):
            return ((i % 2) * 2 + i // 2) * chunk

        def put_down(i, k, v):
            dd[pl.ds(pl.multiple_of(place(i) + k * chunk // 2, chunk // 2), chunk // 2), :] = v

        def put_up(i, k, v):
            du[k * width // 2:(k + 1) * width // 2, pl.ds(pl.multiple_of(place(i), chunk), chunk)] = v

        middle_body(att, hidden, gout, wout, wup, wdown, vecs, ubias, vsum, usum, *scratch[:-1], (o, gm, ga, do), scratch[-1], 0,
                    put_down, put_up, lambda where, i: None)

    return pl.pallas_call(
        kernel,
        out_shape=shapes,
        in_specs=[vm] * 8,
        out_specs=[anyw] * 4 + [vm] * 4,
        scratch_shapes=[pltpu.VMEM((width, tokens), BF), pltpu.VMEM((width, width), BF)] + middle_scratch(tokens, width, chunk) + [pltpu.SemaphoreType.DMA((1 + 3 * (tokens // 256),))],
        compiler_params=pltpu.CompilerParams(vmem_limit_bytes=58 * 1024 * 1024),
        name="middle",
    )(att, hidden.reshape(tokens, width), gout.reshape(tokens, width), wout, wup, wdown, vecs, ubias)


class EarlyReduce:
    SLOTS = 20

    def __init__(self, place, send, recv, g_d, g_u, away_d, away_u, r1_d, r1_u, r2_d, r2_y, r2_x, r3_d):
        self.p, self.send, self.recv = place, send, recv
        self.g_d, self.g_u, self.away_d, self.away_u = g_d, g_u, away_d, away_u
        self.r1_d, self.r1_u, self.r2_d, self.r2_y, self.r2_x, self.r3_d = r1_d, r1_u, r2_d, r2_y, r2_x, r3_d
        self.n = g_d.shape[-1]
        self.h = g_d.shape[-2] // 2

    def copy(self, src, dst, slot, dev):
        return pltpu.make_async_remote_copy(
            src_ref=src, dst_ref=dst, send_sem=self.send.at[slot], recv_sem=self.recv.at[slot], device_id=dev, device_id_type=MESH)

    def mate(self):
        return self.p.at(c=1 - self.p.c)

    def sides(self, v):
        low, high = v[..., :self.n], v[..., self.n:]
        return jnp.where(self.p.c == 0, low, high), jnp.where(self.p.c == 0, high, low)

    def down_core(self, i):
        return self.copy(self.away_d.at[i % 2], self.r1_d.at[i // 2, i % 2], i, self.mate())

    def put_down(self, i, k, v):
        if k == 0:
            @pl.when(i >= 2)
            def _():
                self.down_core(i - 2).wait_send()

        keep, give = self.sides(v.reshape(2, 2 * self.h, 2 * self.n))
        self.g_d[i // 2, i % 2, k] = keep
        self.away_d[i % 2, k] = give

    def down_second(self, t):
        p = self.p
        a, b = pl.ds(0, self.h), pl.ds(self.h, self.h)
        return (self.copy(self.g_d.at[t, 1 - p.y, :, :, a, :], self.r2_d.at[t, 0], 8 + 2 * t, p.at(y=1 - p.y)),
                self.copy(self.g_d.at[t, :, :, 1 - p.x, b, :], self.r2_d.at[t, 1], 9 + 2 * t, p.at(x=1 - p.x)))

    def down_third(self, t):
        p = self.p
        a, b = pl.ds(0, self.h), pl.ds(self.h, self.h)
        return (self.copy(self.g_d.at[t, p.y, :, 1 - p.x, a, :], self.r3_d.at[t, 0], 12 + 2 * t, p.at(x=1 - p.x)),
                self.copy(self.g_d.at[t, 1 - p.y, :, p.x, b, :], self.r3_d.at[t, 1], 13 + 2 * t, p.at(y=1 - p.y)))

    def down_add_core(self, t):
        for y in (0, 1):
            self.down_core(2 * t + y).wait_recv()

        def step(i, _):
            at = (t, i // 4, (i // 2) % 2, i % 2)
            self.g_d[at] = self.g_d[at] + self.r1_d[at]
            return 0

        lax.fori_loop(0, 8, step, 0)
        for copy in self.down_second(t):
            copy.start()

    def down_add_second(self, t):
        p, h = self.p, self.h
        for copy in self.down_second(t):
            copy.wait_recv()

        def step(i, _):
            u, v = i // 2, i % 2
            at, to = (t, p.y, u, v, slice(0, h)), (t, 0, u, v)
            self.g_d[at] = self.g_d[at] + self.r2_d[to]
            at, to = (t, u, v, p.x, slice(h, 2 * h)), (t, 1, u, v)
            self.g_d[at] = self.g_d[at] + self.r2_d[to]
            return 0

        lax.fori_loop(0, 4, step, 0)
        for copy in self.down_third(t):
            copy.start()

    def down_add_third(self, t):
        p, h = self.p, self.h
        for copy in self.down_third(t):
            copy.wait_recv()
        for z in (0, 1):
            for part in (0, 1):
                rows = slice(part * h, (part + 1) * h)
                at = (t, p.y, z, p.x, rows)
                self.g_d[at] = self.g_d[at] + self.r3_d[t, part, z]

    def up_core(self, i):
        return self.copy(self.away_u.at[i % 2], self.r1_u.at[i], 4 + i, self.mate())

    def rows_u(self):
        return self.g_u.shape[-2]

    def put_up(self, i, k, v):
        if k == 0:
            @pl.when(i >= 2)
            def _():
                self.up_core(i - 2).wait_send()

        keep, give = self.sides(v)
        c = pl.ds(pl.multiple_of((i // 2) * self.n, 128), self.n)
        self.g_u[i % 2, k, :, :, :, c] = keep.reshape(4, 2, self.rows_u(), self.n)
        self.away_u[i % 2, k] = give.reshape(4, 2, self.rows_u(), self.n)

    def up_second(self, i):
        p = self.p
        t = i % 2
        c = pl.ds((i // 2) * self.n, self.n)
        if t == 0:
            return self.copy(self.g_u.at[0, 1 - p.y, :, :, :, c], self.r2_y.at[i // 2], 16 + i, p.at(y=1 - p.y))
        return self.copy(self.g_u.at[1, :, :, 1 - p.x, :, c], self.r2_x.at[i // 2], 16 + i, p.at(x=1 - p.x))

    def up_add_core(self, i):
        self.up_core(i).wait_recv()
        c = slice((i // 2) * self.n, (i // 2 + 1) * self.n)

        def step(b, _):
            at = (b // 8, (b // 2) % 4, b % 2)
            here = (i % 2,) + at + (slice(None), c)
            self.g_u[here] = self.g_u[here] + self.r1_u[(i,) + at]
            return 0

        lax.fori_loop(0, 16, step, 0)
        self.up_second(i).start()

    def up_add_second(self, i):
        p = self.p
        self.up_second(i).wait_recv()
        c = slice((i // 2) * self.n, (i // 2 + 1) * self.n)

        def step(b, _):
            if i % 2 == 0:
                here, got = (0, p.y, b // 2, b % 2, slice(None), c), self.r2_y[i // 2, b // 2, b % 2]
            else:
                here, got = (1, b // 4, b % 4, p.x, slice(None), c), self.r2_x[i // 2, b // 4, b % 4]
            self.g_u[here] = self.g_u[here] + got
            return 0

        lax.fori_loop(0, 8, step, 0)

    def left(self):
        for i in (2, 3):
            self.down_core(i).wait_send()
            self.up_core(i).wait_send()
        for t in (0, 1):
            for copy in self.down_second(t) + self.down_third(t):
                copy.wait_send()
        for i in range(4):
            self.up_second(i).wait_send()


def forward_coeffs(s, flags, past, old, ridge, coeffs, coef_t):
    length, basis = past.shape[1], ridge.shape[0]
    samples = ridge.shape[1] - length
    brows = slice(s * basis, (s + 1) * basis)
    diff = (iota((samples, basis), 0) - iota((samples, basis), 1)).astype(F32)
    sampled = jnp.exp(-0.5 * diff * diff).astype(BF)
    keep = (1 - flags[s]).astype(F32)
    old_signal = (dot_nn(sampled, old[s]) * keep).astype(BF)
    co = (dot_nn(ridge[:, :samples], old_signal) + dot_nn(ridge[:, samples:], past[s])).astype(BF)
    coeffs[brows, :] = co
    coef_t[:, brows] = co.T


def forward_projections(s, half, heads, length, basis, hidden, vecs, wmat, wqkv, normed, norm_t, coeffs, qkv, mem, ublk, proj, head_par):
    width = hidden.shape[1]
    hd = width // heads
    rows = slice(s * length, (s + 1) * length)
    brows = slice(s * basis, (s + 1) * basis)
    step = width // 3
    if half == 0:
        unit, _ = norm_parts(hidden[rows, :].astype(F32))
        nrm = (unit * vecs[0:1, :] + vecs[1:2, :]).astype(BF)
        normed[...] = nrm
        norm_t[:, rows] = nrm.T
    for j in range(9) if half == 0 else ():
        cols = slice(j * step, (j + 1) * step)
        y = dot_nn(normed[...], wqkv[:, cols])
        if j < 3:
            y = y + vecs[2:3, cols]
        elif j >= 6:
            y = y + vecs[3:4, (j - 6) * step:(j - 5) * step]
        qkv[rows, cols] = y.astype(BF)
    if half == 0:
        return
    for j in range(6):
        cols = slice(j * step, (j + 1) * step)
        wcols = slice(width + j * step, width + (j + 1) * step)
        mem[brows, cols] = dot_nn(coeffs[brows, :], wqkv[:, wcols]).astype(BF)
    raw = dot_tn(wmat[...], mem[brows, 0:width])[0:32, :]
    own = (iota((32, width), 0) % 16) == (iota((32, width), 1) // hd)
    u = jnp.where(own, raw, 0.0) * (1.0 / math.sqrt(hd))
    ublk[s] = u
    u_hi, u_lo = split_high_low(u)
    q = qkv[rows, 0:width]
    pr = dot_nt(u_hi, q) + dot_nt(u_lo, q)
    proj[s] = pr
    basis_rows(pr, heads, basis, head_par)


def basis_rows(pr, heads, basis, head_par):
    centre = 1.0 / (1.0 + jnp.exp(-pr[0:16]))
    wide = pr[16:32]
    soft = jnp.maximum(wide, 0.0) + jnp.log(1.0 + jnp.exp(-jnp.abs(wide)))
    variance = (soft + 0.5) * 0.02
    inv_root = lax.rsqrt(variance)
    root = inv_root * math.sqrt(0.5 * LOG2E)
    shift_log = jnp.log(inv_root) * LOG2E - math.log2(basis)
    for h in range(heads):
        head_par[h, 0:1, :] = root[h:h + 1]
        head_par[h, 1:2, :] = centre[h:h + 1] * root[h:h + 1]
        head_par[h, 2:3, :] = shift_log[h:h + 1]
    return centre, wide, variance, root


def forward_heads(s, first, last, heads, length, basis, width, qkv, mem, att, lse, head_par, att_t):
    hd = width // heads
    half = length // 2
    rows = slice(s * length, (s + 1) * length)
    brows = slice(s * basis, (s + 1) * basis)
    masks = head_masks(2 * hd, hd)
    scale = LOG2E / math.sqrt(hd)

    def pair(p, _):
        c0 = pl.multiple_of(p * (2 * hd), 2 * hd)
        q = qkv[rows, pl.ds(c0, 2 * hd)]
        k = qkv[rows, pl.ds(pl.multiple_of(width + c0, 2 * hd), 2 * hd)]
        v_t = qkv[rows, pl.ds(pl.multiple_of(2 * width + c0, 2 * hd), 2 * hd)].T
        mv_t = mem[brows, pl.ds(pl.multiple_of(width + c0, 2 * hd), 2 * hd)].T
        cent = ((iota((basis, 1), 0).astype(F32) + 0.5) / basis)
        for h in range(2):
            head = p * 2 + h
            km = k * masks[h]
            lanes = slice(h * hd, (h + 1) * hd)
            for b in range(2):
                cols = slice(b * half, (b + 1) * half)
                depth = (b + 1) * half
                sc = dot_nt(km[:depth], q[cols]) * scale
                allowed = iota((depth, half), 0) <= iota((depth, half), 1) + b * half
                sc = jnp.where(allowed, sc, -1e30)
                top = jnp.max(sc, axis=0, keepdims=True)
                e = jnp.exp2(sc - top)
                total = jnp.sum(e, axis=0, keepdims=True)
                out = dot_nn(v_t[lanes, :depth], e.astype(BF)) / total
                lse[s, head, :, cols] = top + jnp.log(total) * LOG2E
                t = cent * head_par[head, 0:1, cols] - head_par[head, 1:2, cols]
                bas = jnp.exp2(head_par[head, 2:3, cols] - t * t).astype(BF)
                out = out + dot_nn(mv_t[lanes, :], bas)
                att_t[lanes, cols] = out
        att[rows, pl.ds(c0, 2 * hd)] = att_t[...].T.astype(BF)
        return 0

    lax.fori_loop(first, last, pair, 0)


def unpack_small(small, wmat, vecs, ubias, devices, width, ff):
    flat = small.reshape(devices * 32, 128)
    wmat[...] = small.reshape(devices, 32, 128)[:, 0:16, :].reshape(devices * 16, 128)
    every = flat[...]

    def spread(row, offset, each, n):
        pick = (iota((devices, devices * 32), 1) == iota((devices, devices * 32), 0) * 32 + row)
        mine = dot_nn(pick.astype(F32).astype(BF), every).astype(BF)
        place = iota((128, n), 0) == iota((128, n), 1) % each + offset
        wide = dot_nn(mine, place.astype(F32).astype(BF))
        own = iota((devices, n), 1) // each == iota((devices, n), 0)
        return jnp.sum(jnp.where(own, wide, 0.0), axis=0, keepdims=True)

    e = width // devices
    vecs[0:1, :] = spread(16, 0, e, width)
    vecs[1:2, :] = spread(16, e, e, width)
    both = spread(17, 2 * e, 2 * e, 2 * width)
    vecs[2:3, :] = both[:, :width]
    vecs[3:4, :] = both[:, width:]
    vecs[4:5, :] = spread(16, 2 * e, e, width)
    vecs[5:6, :] = spread(16, 3 * e, e, width)
    vecs[6:7, :] = spread(17, 0, e, width)
    vecs[7:8, :] = spread(17, e, e, width)
    up = spread(18, 0, ff // devices, ff)
    chunk = ubias.shape[1]
    ubias[...] = jnp.zeros_like(ubias)
    for j in range(ff // chunk):
        ubias[j:j + 1, :] = up[:, j * chunk:(j + 1) * chunk]


FIRST_STEPS = (
    "#0", "qz1", "qs0", "os0", "qz2", "qs1", "+0", "qz3", "ug", "own", "ot", "qc0", "#1", "qs2", "+1", "qs3", "qc1",
    "uz1", "us0", "oz1", "+2", "uz2", "us1", "oz2", "qc2",
)
LATER_STEPS = (
    ("uz3", "us2", "dg", "oz3", "oc"), ("us3", "uc0", "uc1"), ("dz1",), ("ds0",), ("dz2",), ("ds1",), ("dz3",), ("dc0",),
    (), ("ds2",), (), ("uc2",), ("ds3",), ("dc1",),
)


def forward_kernel(
    heads, devices,
    flags, hidden_h, past_h, old_h, ridge_h, gout_h, small, qkv_s, out_s, up_s, down_s,
    norm_h, coef_h, qkv_h, mem_h, output_h, gmid_h, gatt_h, dout_h, gu_h, gd_h, wq_h,
    lse, ublk, proj, wmat, vecs, vsum, usum,
    hidden, gout, att, wq, wo, wu, wd, ubias,
    wide_s, wide_r, block, block_d, sfull, early, send, recv, local, early_send, early_recv,
):
    place = Place()
    p = place
    tokens, width = hidden.shape
    seqs, length = past_h.shape[0], past_h.shape[1]
    basis = ridge_h.shape[0]
    ff = up_s.shape[1]
    t_qkv, t_out, t_up, t_down = weight_table(width, ff, devices)
    st = Started(send, recv)
    n = Gather.SLOTS
    g_qkv = Gather(place, send, recv, 0, t_qkv, wq)
    g_up = Gather(place, send, recv, n, t_up, wu)
    g_down = Gather(place, send, recv, 2 * n, t_down, wd)
    g_out = LateGather(place, send, recv, 3 * n, t_out, wo)
    base = 4 * n
    nh = wide_r.shape[1]
    blocks = {
        "q": block.at[:, 0:t_qkv.half], "o": block.at[:, t_qkv.half:t_qkv.half + t_out.half],
        "u": block.at[:, t_qkv.half + t_out.half:nh], "d": block_d}
    gather_of = {"q": g_qkv, "o": g_out, "u": g_up, "d": g_down}

    def pass_on(word):
        g, what, n = gather_of[word[0]], word[1], word[2:]
        if what == "g":
            g.start(blocks[word[0]])
        elif what == "z":
            g.on_z(int(n))
        elif what == "s":
            g.on_second(int(n))
        elif what == "t":
            g.on_third()
        elif what == "f":
            g.finish()
        elif n:
            g.core(int(n))
        else:
            g.core()

    stores = []

    def store(src, dst, rows=None):
        i = len(stores)

        def make():
            a, b = (src, dst) if rows is None else (src.at[rows, :], dst.at[rows, :])
            return pltpu.make_async_copy(a, b, local.at[9 + i])

        make().start()
        stores.append(make)

    def attention(norm_t, coef_t, qkv, mem, past, old, ridge, normed, coeffs, head_par, att_t):
        forward_attention(
            heads, devices, place, (flags, hidden_h, past_h, old_h, ridge_h, gout_h, small, qkv_s, out_s, up_s, down_s),
            (t_qkv, t_out, t_up, t_down), st, (g_qkv, g_up, g_down, g_out), base, store, blocks, pass_on,
            (norm_h, coef_h, qkv_h, mem_h, wq_h),
            lse, ublk, proj, wmat, vecs, hidden, gout, norm_t, coef_t, qkv, mem, att, wq, ubias,
            wide_s, wide_r, block, block_d, sfull, local,
            past, old, ridge, normed, coeffs, head_par, att_t)
        for make in stores:
            make().wait()

    pl.run_scoped(
        attention,
        pltpu.VMEM((width, tokens), BF),
        pltpu.VMEM((width, seqs * basis), BF),
        pltpu.VMEM((tokens, 3 * width), BF),
        pltpu.VMEM((seqs * basis, 2 * width), BF),
        pltpu.VMEM(past_h.shape, BF),
        pltpu.VMEM(old_h.shape, BF),
        pltpu.VMEM(ridge_h.shape, BF),
        pltpu.VMEM((length, width), BF),
        pltpu.VMEM((seqs * basis, width), BF),
        pltpu.VMEM((heads, 8, length), F32),
        pltpu.VMEM((2 * (width // heads), length), F32),
    )

    er = EarlyReduce(place, early_send, early_recv, *early)
    sem = 9 + 2 * seqs + 3

    def hook(where, i):
        def at(n, *acts):
            @pl.when(i == n)
            def _():
                for act, arg in acts:
                    act(arg)

        if where == "first":
            er.down_core(i).start()
        elif where == "entered":
            pass_on("uf")
        elif where == "ready":
            for word in ("dc2", "df"):
                pass_on(word)
        elif where == "second":
            er.up_core(i).start()
            at(0, (er.down_add_core, 0))
            at(1, (er.down_add_second, 0))
        elif where == "middle":
            at(2, (er.down_add_core, 1))
            at(3, (er.up_add_core, 2), (er.down_add_third, 0))
        elif where == "both":
            at(0, (er.up_add_core, 0))
            at(1, (er.up_add_core, 1))
        elif where == "leave":
            at(0, (er.up_add_core, 3), (er.down_add_second, 1))
            at(2, (er.up_add_second, 0), (er.up_add_second, 1))
        elif where == "end":
            er.up_add_second(2)
            er.down_add_third(1)
            er.up_add_second(3)

    wflat = wq.reshape(width, 3 * width)

    def feed_forward(*scratch):
        middle_body(
            att, hidden, gout, wo.reshape(width, width), wu.reshape(width, ff), wd.reshape(ff, width), vecs, ubias, vsum, usum,
            wflat.at[:, 0:tokens], wflat.at[:, tokens:tokens + width], *scratch, (output_h, gmid_h, gatt_h, dout_h), local, sem, er.put_down, er.put_up, hook)
        out = [pltpu.make_async_copy(er.g_u, gu_h, local.at[sem + 14])] + [
            pltpu.make_async_copy(er.g_d.at[t, p.y, :, p.x], gd_h.at[2 * t:2 * t + 2], local.at[sem + 15 + t]) for t in (0, 1)]
        for copy in out:
            copy.start()
        er.left()
        for g in (g_up, g_down, g_out):
            g.left()
        for copy in out:
            copy.wait()

    pl.run_scoped(feed_forward, *middle_scratch(tokens, width, ubias.shape[1]))


def forward_attention(
    heads, devices, place, inputs, table, st, gathers, base, store, blocks, pass_on, outs,
    lse, ublk, proj, wmat, vecs, hidden, gout, norm_t, coef_t, qkv, mem, att, wq, ubias,
    wide_s, wide_r, block, block_d, sfull, local,
    past, old, ridge, normed, coeffs, head_par, att_t,
):
    p = place
    flags, hidden_h, past_h, old_h, ridge_h, gout_h, small, qkv_s, out_s, up_s, down_s = inputs
    t_qkv, t_out, t_up, t_down = table
    g_qkv, g_up, g_down, g_out = gathers
    norm_h, coef_h, qkv_h, mem_h, wq_h = outs
    tokens, width = hidden.shape
    seqs, length = past.shape[0], past.shape[1]
    basis = ridge.shape[0]
    ff = up_s.shape[1]
    loads = []
    for i, (src, dst) in enumerate(((ridge_h, ridge), (old_h, old), (past_h, past), (hidden_h, hidden), (gout_h, gout))):
        copy = pltpu.make_async_copy(src, dst, local.at[i])
        copy.start()
        loads.append(copy)
    pos = 0
    for half in range(2):
        for ref, w in ((qkv_s, t_qkv), (out_s, t_out), (up_s, t_up)):
            wide_s[:, pos:pos + w.half] = ref[:, half * w.half:(half + 1) * w.half].astype(F32)
            pos += w.half
    nh = pos // 2
    sfull[p.y, p.z, p.x, p.c] = small[...]
    ed = down_s.shape[0]
    hd_cols = width // 2
    block_d[pl.ds(pl.multiple_of(p.c * ed, 16), ed), :] = down_s[:, pl.ds(pl.multiple_of(p.c * hd_cols, 128), hd_cols)]

    place.greet(place.others())
    mate = p.at(c=1 - p.c)
    there = pl.multiple_of((1 - p.c) * nh, 128)
    st.go("wide", wide_s.at[:, pl.ds(there, t_qkv.half)], wide_r.at[:, 0:t_qkv.half], base, mate)
    st.go("wide2", wide_s.at[:, pl.ds(pl.multiple_of(there + t_qkv.half, 128), nh - t_qkv.half)], wide_r.at[:, t_qkv.half:nh], base + 8, mate)
    ref = sfull.at[p.y, p.z, p.x, p.c]
    st.go("s0", ref, ref, base + 1, mate)
    st.go("down", down_s.at[:, pl.ds(pl.multiple_of((1 - p.c) * hd_cols, 128), hd_cols)],
          block_d.at[pl.ds(pl.multiple_of(p.c * ed, 16), ed), :], base + 2, mate)

    def make_block(c0, cn):
        mine = wide_s[:, pl.ds(pl.multiple_of(p.c * nh + c0, 128), cn)]
        other = wide_r[:, c0:c0 + cn]
        block[:, c0:c0 + cn] = jnp.concatenate(
            [jnp.where(p.c == 0, mine, other), jnp.where(p.c == 0, other, mine)], axis=0).astype(BF)

    b_qkv, b_out, b_up = blocks["q"], blocks["o"], blocks["u"]
    own = []

    def keep_own(g, src, i):
        copy = pltpu.make_async_copy(src, g.full.at[p.y, p.z, p.x, :, g.w.columns(p.c)], local.at[i])
        copy.start()
        own.append(copy)

    st.arrived("wide")
    make_block(0, t_qkv.half)
    g_qkv.start(b_qkv)
    st.arrived("s0")
    ref = sfull.at[p.y, p.z, p.x]
    for s in (1, 2, 3):
        st.go("sz", ref, ref, base + 2 + s, p.at(z=p.far_z(s)))
    st.arrived("wide2")
    make_block(t_qkv.half, nh - t_qkv.half)
    g_out.start(b_out)
    st.arrived("down")
    for i, (g, src) in enumerate(((g_qkv, b_qkv), (g_out, b_out), (g_up, b_up), (g_down, block_d))):
        keep_own(g, src, 5 + i)
    loads[0].wait()
    loads[1].wait()
    loads[2].wait()
    def small_step(i):
        if i == 0:
            st.arrived("sz")
            ref = sfull.at[p.y, :, p.x]
            st.go("sx", ref, ref, base + 6, p.at(x=1 - p.x))
        elif i == 1:
            st.arrived("sx")
            ref = sfull.at[p.y]
            st.go("sy", ref, ref, base + 7, p.at(y=1 - p.y))
        else:
            st.arrived("sy")
            unpack_small(sfull, wmat, vecs, ubias, devices, width, ff)

    def own_in_place():
        for copy in own:
            copy.wait()

    def perform(word):
        if word == "own":
            own_in_place()
        elif word[0] == "#":
            forward_coeffs(int(word[1]), flags, past, old, ridge, coeffs, coef_t)
        elif word[0] == "+":
            small_step(int(word[1]))
        else:
            pass_on(word)

    for word in FIRST_STEPS:
        perform(word)
    loads[3].wait()
    g_qkv.finish()
    wflat = wq.reshape(width, 3 * width)
    store(wq, wq_h)
    store(coef_t, coef_h)

    def project(s, half):
        forward_projections(s, half, heads, length, basis, hidden, vecs, wmat, wflat, normed, norm_t, coeffs, qkv, mem, ublk, proj, head_par)

    def attend(s, a, b):
        forward_heads(s, a, b, heads, length, basis, width, qkv, mem, att, lse, head_par, att_t)

    events = iter(LATER_STEPS)

    def step(count=1):
        for _ in range(count):
            for word in next(events, ()):
                perform(word)

    pairs = heads // 2
    for s in range(seqs):
        project(s, 0)
        step()
        project(s, 1)
        store(qkv, qkv_h, slice(s * length, (s + 1) * length))
        store(mem, mem_h, slice(s * basis, (s + 1) * basis))
        if s == seqs - 1:
            store(norm_t, norm_h)
        step()
        for a in range(pairs):
            attend(s, a, a + 1)
            step()
    step(99)
    g_out.finish()
    loads[4].wait()
    st.left()
    g_qkv.left()


def forward_call(heads, devices, flags, hidden, past, old, ridge, gout, small, qkv_s, out_s, up_s, down_s):
    seqs, length, width = hidden.shape
    basis = ridge.shape[0]
    tokens = seqs * length
    ff = up_s.shape[1]
    chip = 2 * width // devices
    chip_ff = 2 * ff // devices
    vm = pl.BlockSpec(memory_space=pltpu.VMEM)
    anyw = pl.BlockSpec(memory_space=pl.ANY)
    full = (2, 4, 2, chip, 3 * width)
    n = width // 2
    far = [
        ((width, tokens), BF), ((width, seqs * basis), BF), ((tokens, 3 * width), BF), ((seqs * basis, 2 * width), BF),
        ((tokens, width), BF), ((tokens, width), F32), ((tokens, width), BF),
        ((width, width), BF), ((2, 2, 4, 2, chip, 2 * n), BF), ((4, chip_ff, n), BF), (full, BF)]
    near = [
        ((seqs, heads, 1, length), F32), ((seqs, 32, width), F32), ((seqs, 32, length), F32),
        ((basis, 128), BF), ((8, width), F32), ((8, width), F32), ((8, width), F32)]
    nh = (4 * width + ff) // 2
    slots = 4 * Gather.SLOTS + 9
    return pl.pallas_call(
        lambda *refs: forward_kernel(heads, devices, *refs),
        out_shape=tuple(jax.ShapeDtypeStruct(*m) for m in far + near),
        in_specs=[pl.BlockSpec(memory_space=pltpu.SMEM)] + [anyw] * 5 + [vm] * 5,
        out_specs=[anyw] * len(far) + [vm] * len(near),
        scratch_shapes=[
            pltpu.VMEM((tokens, width), BF),
            pltpu.VMEM((tokens, width), BF),
            pltpu.VMEM((tokens, width), BF),
            pltpu.VMEM(full, BF),
            pltpu.VMEM((2, 4, 2, chip, width), BF),
            pltpu.VMEM((2, 4, 2, chip, ff), BF),
            pltpu.VMEM((2, 4, 2, chip_ff, width), BF),
            pltpu.VMEM((8, width), F32),
            pltpu.VMEM((width // devices, 2 * nh), F32),
            pltpu.VMEM((width // devices, nh), F32),
            pltpu.VMEM((chip, nh), BF),
            pltpu.VMEM((chip_ff, width // 2), BF),
            pltpu.VMEM((2, 4, 2, 2, 32, 128), BF),
            [pltpu.VMEM(shape, BF) for shape in (
                (2, 2, 2, 2, chip_ff, n), (2, 2, 4, 2, chip, 2 * n), (2, 2, 2, chip_ff, n), (2, 2, 4, 2, chip, n),
                (2, 2, 2, 2, chip_ff, n), (4, 2, 4, 2, chip, n),
                (2, 2, 2, 2, chip_ff // 2, n), (2, 4, 2, chip, n), (2, 2, 4, chip, n), (2, 2, 2, chip_ff // 2, n))],
            pltpu.SemaphoreType.DMA((slots,)),
            pltpu.SemaphoreType.DMA((slots,)),
            pltpu.SemaphoreType.DMA((9 + 2 * seqs + 3 + 17,)),
            pltpu.SemaphoreType.DMA((EarlyReduce.SLOTS,)),
            pltpu.SemaphoreType.DMA((EarlyReduce.SLOTS,)),
        ],
        compiler_params=pltpu.CompilerParams(vmem_limit_bytes=61 * 1024 * 1024, collective_id=0, has_side_effects=True),
        name="forward",
    )(flags, hidden.reshape(tokens, width), past, old, ridge, gout.reshape(tokens, width), small, qkv_s, out_s, up_s, down_s)


def forward_plain_call(heads, flags, hidden, past, old, ridge, wmat, vecs, wqkv):
    seqs, length, width = hidden.shape
    basis = ridge.shape[0]
    tokens = seqs * length
    vm = pl.BlockSpec(memory_space=pltpu.VMEM)

    def kernel(
        flags, hidden, past, old, ridge, wmat, vecs, wqkv,
        norm_t, coef_t, qkv, mem, att, lse, ublk, proj, normed, coeffs, head_par, att_t,
    ):
        for s in range(seqs):
            forward_coeffs(s, flags, past, old, ridge, coeffs, coef_t)
            for half in (0, 1):
                forward_projections(s, half, heads, length, basis, hidden, vecs, wmat, wqkv, normed, norm_t, coeffs, qkv, mem, ublk, proj, head_par)
            forward_heads(s, 0, heads // 2, heads, length, basis, width, qkv, mem, att, lse, head_par, att_t)

    shapes = (
        jax.ShapeDtypeStruct((width, tokens), BF),
        jax.ShapeDtypeStruct((width, seqs * basis), BF),
        jax.ShapeDtypeStruct((tokens, 3 * width), BF),
        jax.ShapeDtypeStruct((seqs * basis, 2 * width), BF),
        jax.ShapeDtypeStruct((tokens, width), BF),
        jax.ShapeDtypeStruct((seqs, heads, 1, length), F32),
        jax.ShapeDtypeStruct((seqs, 32, width), F32),
        jax.ShapeDtypeStruct((seqs, 32, length), F32),
    )
    return pl.pallas_call(
        kernel,
        out_shape=shapes,
        in_specs=[pl.BlockSpec(memory_space=pltpu.SMEM)] + [vm] * 7,
        out_specs=[vm] * 8,
        scratch_shapes=[
            pltpu.VMEM((length, width), BF),
            pltpu.VMEM((seqs * basis, width), BF),
            pltpu.VMEM((heads, 8, length), F32),
            pltpu.VMEM((2 * (width // heads), length), F32),
        ],
        compiler_params=pltpu.CompilerParams(vmem_limit_bytes=VMEM_BYTES),
        name="forward_plain",
    )(flags, hidden.reshape(tokens, width), past, old, ridge, wmat, vecs, wqkv)


def backward_heads(s, p, first, heads, length, basis, width, qkv, mem, gatt, lse, head_par, grows, dq_t, gqkv, gmem):
    hd = width // heads
    half = length // 2
    rows = slice(s * length, (s + 1) * length)
    brows = slice(s * basis, (s + 1) * basis)
    masks = head_masks(2 * hd, hd)
    scale = LOG2E / math.sqrt(hd)
    c0 = pl.multiple_of(p * (2 * hd), 2 * hd)
    c1 = pl.multiple_of(width + c0, 2 * hd)
    c2 = pl.multiple_of(2 * width + c0, 2 * hd)
    here = pl.multiple_of((p - first) * (2 * hd), 2 * hd)
    wide = gmem.shape[1] // 2
    q = qkv[rows, pl.ds(c0, 2 * hd)]
    k = qkv[rows, pl.ds(c1, 2 * hd)]
    v = qkv[rows, pl.ds(c2, 2 * hd)]
    mv = mem[brows, pl.ds(c1, 2 * hd)]
    ga = gatt[rows, pl.ds(c0, 2 * hd)]
    k_t = k.T
    cent = ((iota((basis, 1), 0).astype(F32) + 0.5) / basis)
    dv = [0.0, 0.0]
    dk = [0.0, 0.0]
    dmv = 0.0
    for h in range(2):
        head = p * 2 + h
        km, vm, mvm, gam, qm = (a * masks[h] for a in (k, v, mv, ga, q))
        lanes = slice(h * hd, (h + 1) * hd)
        for b in range(2):
            cols = slice(b * half, (b + 1) * half)
            depth = (b + 1) * half
            sc = dot_nt(km[:depth], q[cols]) * scale
            pr = jnp.exp2(sc - lse[s, head, :, cols])
            allowed = iota((depth, half), 0) <= iota((depth, half), 1) + b * half
            pr = jnp.where(allowed, pr, 0.0)
            dp = dot_nt(vm[:depth], ga[cols])
            inner = jnp.sum(pr * dp, axis=0, keepdims=True)
            ds = (pr * (dp - inner)).astype(BF)
            pb = pr.astype(BF)
            dvb = dot_nn(pb, gam[cols])
            dkb = dot_nn(ds, qm[cols])
            dq_t[pl.ds(pl.multiple_of(here + h * hd, hd), hd), cols] = dot_nn(k_t[lanes, :depth], ds)
            for i in range(b + 1):
                part = slice(i * half, (i + 1) * half)
                dv[i] = dv[i] + dvb[part]
                dk[i] = dk[i] + dkb[part]
            t = cent * head_par[head, 0:1, cols] - head_par[head, 1:2, cols]
            bas = jnp.exp2(head_par[head, 2:3, cols] - t * t)
            e = dot_nt(mvm, ga[cols]) * bas
            et = e * t
            grows[0, pl.ds(head, 1), cols] = jnp.sum(e, axis=0, keepdims=True)
            grows[1, pl.ds(head, 1), cols] = jnp.sum(et, axis=0, keepdims=True)
            grows[2, pl.ds(head, 1), cols] = jnp.sum(et * t, axis=0, keepdims=True)
            dmv = dmv + dot_nn(bas.astype(BF), gam[cols])
    for i in range(2):
        out_rows = slice(s * length + i * half, s * length + (i + 1) * half)
        gqkv[out_rows, pl.ds(c1, 2 * hd)] = (dk[i] * (1.0 / math.sqrt(hd))).astype(BF)
        gqkv[out_rows, pl.ds(c2, 2 * hd)] = dv[i].astype(BF)
    gmem[brows, pl.ds(pl.multiple_of(wide + here, 2 * hd), 2 * hd)] = dmv.astype(BF)


def backward_finish(s, start, heads, rows_of, qkv, mem, ublk, grows, dq_t, wmat, gqkv, gmem, msum):
    centre, wide, variance, root = rows_of
    n, length = dq_t.shape
    width = ublk.shape[2]
    basis = wmat.shape[0]
    hd = width // heads
    rows = slice(s * length, (s + 1) * length)
    brows = slice(s * basis, (s + 1) * basis)
    cols = slice(start, start + n)
    inv_var = 1.0 / variance
    s0, s1, s2 = grows[0], grows[1], grows[2]
    to_centre = s1 * (inv_var / root) * centre * (1.0 - centre)
    wide_slope = 0.02 / (1.0 + jnp.exp(-wide))
    to_wide = (-0.5 * s0 * inv_var + s2 * (0.5 * inv_var * inv_var) / (root * root)) * wide_slope
    head = iota((16, length), 0)
    live = (head >= start // hd) & (head < (start + n) // hd)
    g = jnp.concatenate([jnp.where(live, to_centre, 0.0), jnp.where(live, to_wide, 0.0)], axis=0)
    g_hi, g_lo = split_high_low(g)
    u_hi, u_lo = split_high_low(ublk[s, :, cols])
    dqm = dot_tn(u_hi, g_hi) + dot_tn(u_hi, g_lo) + dot_tn(u_lo, g_hi)
    total = dq_t[...] * (1.0 / math.sqrt(hd)) + dqm
    gqkv[rows, cols] = total.T.astype(BF)
    q = qkv[rows, cols]
    own = (iota((32, n), 0) % 16) == (iota((32, n), 1) + start) // hd
    r = dot_nn(g_hi, q) + dot_nn(g_lo, q)
    r = jnp.where(own, r, 0.0) * (1.0 / math.sqrt(hd))
    r_hi, r_lo = split_high_low(r)
    w = wmat[...][:, 0:32]
    gmem[brows, 0:n] = (dot_nn(w, r_hi) + dot_nn(w, r_lo)).astype(BF)
    mk = mem[brows, cols]
    add = dot_nt(r_hi, mk) + dot_nt(r_lo, mk)
    if msum.shape[0] == 32:
        msum[...] += add
    else:
        some, at = n // hd, start // hd
        msum[...] += jnp.concatenate([add[at:at + some], add[16 + at:16 + at + some]], axis=0)


def backward_input(r, width, hid, gm, gqkv, wqkv, vecs, gin, vsum):
    g = dot_nt(gqkv[r, :], wqkv[...])
    unit, inv = norm_parts(hid.astype(F32))
    gin[...] = (gm + norm_back(g, unit, inv, vecs[0:1, :])).astype(BF)
    vsum[0:1, :] += jnp.sum(g * unit, axis=0, keepdims=True)
    vsum[1:2, :] += jnp.sum(g, axis=0, keepdims=True)


def bias_sums(width, gqkv, out):
    out[0:1, :] = jnp.sum(gqkv[:, 0:width].astype(F32), axis=0, keepdims=True)
    out[1:2, :] = jnp.sum(gqkv[:, 2 * width:3 * width].astype(F32), axis=0, keepdims=True)


def backward_plain_call(heads, hidden, norm_t, coef_t, qkv, mem, gatt, gmid, lse, ublk, proj, wmat, vecs, wqkv):
    seqs, length, width = hidden.shape
    tokens = seqs * length
    brows = coef_t.shape[1]
    basis = brows // seqs
    vm = pl.BlockSpec(memory_space=pltpu.VMEM)

    def kernel(
        hidden, norm_t, coef_t, qkv, mem, gatt, gmid, lse, ublk, proj, wmat, vecs, wqkv,
        gin, dqkv, vsum, msum, gqkv, gmem, head_par, grows, dq_t,
    ):
        vsum[...] = jnp.zeros_like(vsum)
        msum[...] = jnp.zeros_like(msum)
        grows[...] = jnp.zeros_like(grows)
        for s in range(seqs):
            rows_of = basis_rows(proj[s], heads, basis, head_par)

            def pair(p, _):
                backward_heads(s, p, 0, heads, length, basis, width, qkv, mem, gatt, lse, head_par, grows, dq_t, gqkv, gmem)
                return 0

            lax.fori_loop(0, heads // 2, pair, 0)
            backward_finish(s, 0, heads, rows_of, qkv, mem, ublk, grows, dq_t, wmat, gqkv, gmem, msum)
        step = width // 3
        for j in range(9):
            c = slice(j * step, (j + 1) * step)
            y = dot_nn(norm_t[...], gqkv[:, c])
            if j >= 3:
                y = y + dot_nn(coef_t[...], gmem[:, (j - 3) * step:(j - 2) * step])
            dqkv[:, c] = y.astype(BF)

        def last(i, _):
            r = pl.ds(pl.multiple_of(i * 256, 256), 256)
            backward_input(r, width, hidden[r, :], gmid[r, :], gqkv, wqkv, vecs, gin.at[r, :], vsum.at[2:4, :])
            return 0

        lax.fori_loop(0, tokens // 256, last, 0)
        bias_sums(width, gqkv, vsum)

    shapes = (
        jax.ShapeDtypeStruct((tokens, width), BF),
        jax.ShapeDtypeStruct((width, 3 * width), BF),
        jax.ShapeDtypeStruct((8, width), F32),
        jax.ShapeDtypeStruct((32, basis), F32),
    )
    return pl.pallas_call(
        kernel,
        out_shape=shapes,
        in_specs=[vm] * 13,
        out_specs=[vm] * 4,
        scratch_shapes=[
            pltpu.VMEM((tokens, 3 * width), BF),
            pltpu.VMEM((brows, 2 * width), BF),
            pltpu.VMEM((heads, 8, length), F32),
            pltpu.VMEM((3, 16, length), F32),
            pltpu.VMEM((width, length), F32),
        ],
        compiler_params=pltpu.CompilerParams(vmem_limit_bytes=VMEM_BYTES),
        name="backward_plain",
    )(hidden.reshape(tokens, width), norm_t, coef_t, qkv, mem, gatt, gmid, lse, ublk, proj, wmat, vecs, wqkv)


class Reduce:
    SLOTS = 13

    def __init__(self, place, started, name, base, parts, bufs):
        self.p, self.s, self.name, self.base, self.parts = place, started, name, base, parts
        self.g, self.r1, self.r2, self.r3, self.r4, self.f = bufs

    def where(self, part):
        r0, rn, c0, cn = self.parts[part]
        return pl.ds(r0, rn), pl.ds(c0, cn)

    def core(self, *pieces):
        for i, (src, rows) in enumerate(pieces):
            self.s.go((self.name, 1), src, self.r1.at[:, :, :, rows, :], self.base + i, self.p.at(c=1 - self.p.c))

    def second(self):
        p = self.p
        self.s.arrived((self.name, 1))

        def step(i, _):
            at = (i // 8, (i // 2) % 4, i % 2)
            self.g[at] = self.g[at] + self.r1[at]
            return 0

        lax.fori_loop(0, 16, step, 0)
        for part in (0, 1):
            r, c = self.where(part)
            if part == 0:
                self.s.go((self.name, 2), self.g.at[1 - p.y, :, :, r, c], self.r2[0], self.base + 2, p.at(y=1 - p.y))
            else:
                self.s.go((self.name, 2), self.g.at[:, :, 1 - p.x, r, c], self.r2[1], self.base + 3, p.at(x=1 - p.x))

    def third(self):
        p = self.p
        self.s.arrived((self.name, 2))
        r, c = self.where(0)
        r_b, c_b = self.where(1)

        def step(i, _):
            z, k = i // 2, i % 2
            self.g[p.y, z, k, r, c] = self.g[p.y, z, k, r, c] + self.r2[0][z, k]
            self.g[k, z, p.x, r_b, c_b] = self.g[k, z, p.x, r_b, c_b] + self.r2[1][k, z]
            return 0

        lax.fori_loop(0, 8, step, 0)
        for part in (0, 1):
            self.send_third(part)

    def send_third(self, part):
        p = self.p
        r, c = self.where(part)
        if part == 0:
            self.s.go((self.name, 3), self.g.at[p.y, :, 1 - p.x, r, c], self.r3[0], self.base + 4, p.at(x=1 - p.x))
        else:
            self.s.go((self.name, 3), self.g.at[1 - p.y, :, p.x, r, c], self.r3[1], self.base + 5, p.at(y=1 - p.y))

    def along(self):
        p = self.p
        self.s.arrived((self.name, 3))

        def step(z, _):
            for part in self.parts:
                r, c = self.where(part)
                self.g[p.y, z, p.x, r, c] = self.g[p.y, z, p.x, r, c] + self.r3[part][z]
            return 0

        lax.fori_loop(0, 4, step, 0)
        self.send_along()

    def summand(self, z):
        p = self.p
        return self.g.at[z] if len(self.g.shape) == 3 else self.g.at[p.y, z, p.x]

    def send_along(self):
        p = self.p
        for s in (1, 2, 3):
            to = p.far_z(s)
            self.s.go((self.name, 4), self.summand(to), self.r4.at[s - 1], self.base + 5 + s, p.at(z=to))

    def last(self, out, segments):
        p = self.p
        self.s.arrived((self.name, 4))
        own = self.summand(p.z)[...].astype(F32)
        self.f[...] = (own + self.r4[0].astype(F32)) + (self.r4[1].astype(F32) + self.r4[2].astype(F32))
        n = self.f.shape[0] // 2
        theirs = pl.ds(pl.multiple_of((1 - p.c) * n, 8), n)
        mine = pl.ds(pl.multiple_of(p.c * n, 8), n)
        for i, (c0, to, cn) in enumerate(segments):
            there = out.at[:, pl.ds(pl.multiple_of(to, 128), cn)]
            self.s.go((self.name, 5), self.f.at[theirs, pl.ds(c0, cn)], there, self.base + 9 + i, p.at(c=1 - p.c))
            there[...] = self.f[mine, c0:c0 + cn]

    def done(self):
        self.s.arrived((self.name, 5))


class Everywhere:
    SLOTS = 10

    def __init__(self, place, started, name, slot, held, got):
        self.p, self.s, self.name, self.slot, self.held, self.got = place, started, name, slot, held, got

    def start(self, step):
        p = self.p
        if step == 0:
            for d in range(1, 8):
                to = p.at(y=(p.y + d // 4) % 2, x=(p.x + d // 2) % 2, c=(p.c + d) % 2)
                self.s.go((self.name, 0), self.held.at[0], self.got.at[d - 1], self.slot + d - 1, to)
        else:
            for s in (1, 2, 3):
                self.s.go((self.name, 1), self.held.at[1], self.got.at[6 + s], self.slot + 6 + s, p.at(z=p.far_z(s)))

    def add(self, step):
        self.s.arrived((self.name, step))
        first = 0 if step == 0 else 7
        total = self.held[step]
        for i in range(first, 7 if step == 0 else 10):
            total = total + self.got[i]
        if step == 0:
            self.held[1] = total
        return total


BACK_STEPS = (
    (), (), ("a3", "b3", "o1"), ("e0",),
    ("u0", "o2"), ("p1", "d4"), ("e1", "p2"), ("u1", "o3", "a4"),
    ("q1",), ("p3", "b4", "v0"), ("q2",), ("p4", "o4"),
    ("r1", "v1"), ("k0", "w0", "q3"), (), ("r2", "w1", "k1"),
    ("l0",), ("r3",), ("l1",), ("q4",), ("r4",),
)


def backward_kernel(
    heads, devices,
    hidden, norm_h, coef_h, qkv_h, mem_h, gatt_h, gmid, lse, ublk, proj, wmat, vecs, vsum_a, usum, wq_h, p_out, gu_h, gd_h,
    gin, o_qkv, o_out, o_up, o_down, early, late, msum,
    norm_t, coef_t, qkv, mem, gatt, wq,
    gqkv, gmem, head_par, grows, dq_t, away, gm_buf, hid_buf, gin_buf,
    bufs, vsum, e_held, e_got, l_held, l_got, k_held, k_got, m_held, m_got, send, recv, local,
):
    place = Place()
    p = place
    tokens, width = hidden.shape
    seqs, _, length = proj.shape
    basis = wmat.shape[0]
    ff = o_up.shape[1]
    st = Started(send, recv)
    names = "abdopqr"
    red = {n: Reduce(place, st, n, i * Reduce.SLOTS, parts, bufs[i]) for i, (n, (_, _, parts)) in enumerate(zip(names, reduce_shapes(width, ff, devices)))}
    base = len(names) * Reduce.SLOTS
    sums = {"e": Everywhere(place, st, "e", base, e_held, e_got), "l": Everywhere(place, st, "l", base + Everywhere.SLOTS, l_held, l_got)}
    sums["k"] = Everywhere(place, st, "k", base + 5 * Everywhere.SLOTS, k_held, k_got)
    for i, n in enumerate("uvw"):
        sums[n] = Everywhere(place, st, n, base + (2 + i) * Everywhere.SLOTS, m_held.at[i], m_got.at[i])
    loads = []
    for i, (src, dst) in enumerate(((qkv_h, qkv), (mem_h, mem), (gatt_h, gatt), (norm_h, norm_t), (coef_h, coef_t), (wq_h, wq))):
        copy = pltpu.make_async_copy(src, dst, local.at[i])
        copy.start()
        loads.append(copy)
    grows[...] = jnp.zeros_like(grows)
    vsum[...] = jnp.zeros_like(vsum)
    e_held[0] = jnp.concatenate([vsum_a[...], usum[...]], axis=0)
    half = width // 2

    def side(c):
        return p_out.at[:, :, :, :, pl.ds(pl.multiple_of(c * half, 128), half)]

    own = [pltpu.make_async_copy(src, red[n].g, local.at[6 + i])
           for i, (n, src) in enumerate((("a", gu_h.at[0]), ("b", gu_h.at[1]), ("d", gd_h), ("o", side(p.c))))]
    for copy in own:
        copy.start()
    place.greet(place.layer())
    red["o"].core((side(1 - p.c), slice(None)))
    sums["e"].start(0)
    for copy in own:
        copy.wait()
    red["d"].send_along()
    red["a"].send_third(0)
    red["b"].send_third(1)
    pieces = 128
    outs = {
        "a": (o_up, lambda: [(k * half, k * width + p.c * half, half) for k in (0, 1)]),
        "b": (o_up, lambda: [(k * half, (2 + k) * width + p.c * half, half) for k in (0, 1)]),
        "d": (o_down, lambda: [(0, p.c * half, half)]),
        "o": (o_out, lambda: [(0, p.c * half, half)]),
    }
    for i, n in enumerate("pqr"):
        outs[n] = (o_qkv, lambda i=i: [(j * pieces, j * width + i * 2 * pieces + p.c * pieces, pieces) for j in range(3)])

    def perform(word):
        if word[0] in sums:
            total, step = sums[word[0]], int(word[1])
            value = total.add(step)
            if step == 0:
                total.start(1)
            else:
                if word[0] in "uvw":
                    n = value.shape[0]
                    msum["uvw".index(word[0]) * n:("uvw".index(word[0]) + 1) * n, :] = value
                else:
                    {"e": early, "l": late.at[0:2, :], "k": late.at[2:4, :]}[word[0]][...] = value
        else:
            r, step = red[word[0]], word[1]
            if step == "1":
                r.second()
            elif step == "2":
                r.third()
            elif step == "3":
                r.along()
            else:
                out, segments = outs[word[0]]
                r.last(out, segments())

    steps = iter(BACK_STEPS)

    def advance():
        for word in next(steps, ()):
            perform(word)

    for copy in loads[:3]:
        copy.wait()
    chunk = 2 * pieces
    m_held[...] = jnp.zeros_like(m_held)
    rows_of = [basis_rows(proj[s], heads, basis, head_par.at[s]) for s in range(seqs)]
    for i in range(3):
        for s in range(seqs):
            for k in range(2):
                def one(j, _):
                    backward_heads(s, j, 2 * i, heads, length, basis, width, qkv, mem, gatt, lse, head_par.at[s], grows, dq_t, gqkv, gmem)
                    return 0

                lax.fori_loop(2 * i + k, 2 * i + k + 1, one, 0)
                if k == 0:
                    advance()
            backward_finish(s, i * chunk, heads, rows_of[s], qkv, mem, ublk, grows, dq_t, wmat, gqkv, gmem, m_held.at[i, 0])
            if s < seqs - 1:
                advance()
        if i == 0:
            loads[3].wait()
            loads[4].wait()
        r = red["pqr"[i]]
        for j in range(3):
            c = j * width + i * chunk
            y = dot_nn(norm_t[...], gqkv[:, c:c + chunk])
            if j > 0:
                y = y + dot_nn(coef_t[...], gmem[:, (j - 1) * chunk:j * chunk])
            y = y.astype(BF).reshape(2, 4, 2, r.g.shape[3], chunk)
            low, high = y[..., :pieces], y[..., pieces:]
            keep, give = jnp.where(p.c == 0, low, high), jnp.where(p.c == 0, high, low)
            r.g[:, :, :, :, j * pieces:(j + 1) * pieces] = keep
            away[i, :, :, :, :, j * pieces:(j + 1) * pieces] = give
        r.core((away.at[i], slice(None)))
        sums["uvw"[i]].start(0)
        if i == 2:
            bias_sums(width, gqkv, k_held.at[0])
            sums["k"].start(0)
        advance()
    wflat = wq.reshape(width, 3 * width)
    loads[5].wait()
    blocks = tokens // 256

    def fetch(i):
        r = slice(i * 256, (i + 1) * 256)
        return (pltpu.make_async_copy(gmid.at[r, :], gm_buf.at[i % 2], local.at[16 + i % 2]),
                pltpu.make_async_copy(hidden.at[r, :], hid_buf.at[i % 2], local.at[18 + i % 2]))

    def emit(i):
        return pltpu.make_async_copy(gin_buf.at[i % 2], gin.at[i * 256:(i + 1) * 256, :], local.at[20 + i % 2])

    for i in (0, 1):
        for copy in fetch(i):
            copy.start()
    for i in range(blocks):
        for copy in fetch(i):
            copy.wait()
        if i >= 2:
            emit(i - 2).wait()
        backward_input(slice(i * 256, (i + 1) * 256), width, hid_buf[i % 2], gm_buf[i % 2], gqkv, wflat, vecs, gin_buf.at[i % 2], vsum)
        emit(i).start()
        if i + 2 < blocks:
            for copy in fetch(i + 2):
                copy.start()
        if i == blocks - 1:
            l_held[0] = vsum[...]
            sums["l"].start(0)
        advance()
    for _ in range(99):
        advance()
    for n in names:
        red[n].done()
    for i in (blocks - 2, blocks - 1):
        emit(i).wait()
    st.left()


def reduce_shapes(width, ff, devices):
    chip, chip_ff = 2 * width // devices, 2 * ff // devices
    h = width // 2
    more = (chip, h, {0: (0, chip, 0, 256), 1: (0, chip, 256, 128)})
    less = (chip, h, {0: (0, chip, 0, 128), 1: (0, chip, 128, 256)})
    return [(chip, width, {0: (0, chip, 0, width)}), (chip, width, {1: (0, chip, 0, width)}), (chip_ff, h, {}), more, less, more, less]


def backward_call(
    heads, devices, hidden, norm_t, coef_t, qkv, mem, gatt, gmid, lse, ublk, proj, wmat, vecs, vsum_a, usum, wq, p_out, g_up, g_down, ff,
):
    seqs, length, width = hidden.shape
    tokens = seqs * length
    brows = coef_t.shape[1]
    basis = brows // seqs
    vm = pl.BlockSpec(memory_space=pltpu.VMEM)
    anyw = pl.BlockSpec(memory_space=pl.ANY)
    shapes = (
        jax.ShapeDtypeStruct((tokens, width), BF),
        jax.ShapeDtypeStruct((width // devices, 3 * width), F32),
        jax.ShapeDtypeStruct((width // devices, width), F32),
        jax.ShapeDtypeStruct((width // devices, ff), F32),
        jax.ShapeDtypeStruct((ff // devices, width), F32),
        jax.ShapeDtypeStruct((16, width), F32),
        jax.ShapeDtypeStruct((4, width), F32),
        jax.ShapeDtypeStruct((24, basis), F32),
    )

    def buffers(i, shape):
        rows, cols, parts = shape
        none = pltpu.VMEM((8, 128), F32)
        whole = i > 2
        sizes = [parts.get(k, (0, 16, 0, 128)) for k in (0, 1)]
        (_, ra, _, ca), (_, rb, _, cb) = sizes
        return (
            pltpu.VMEM((4, rows, cols) if i == 2 else (2, 4, 2, rows, cols), BF),
            pltpu.VMEM((2, 4, 2, rows, cols), BF) if whole else none,
            (pltpu.VMEM((4, 2, ra, ca), BF), pltpu.VMEM((2, 4, rb, cb), BF)) if whole else (none, none),
            (pltpu.VMEM((4, ra, ca), BF), pltpu.VMEM((4, rb, cb), BF)),
            pltpu.VMEM((3, rows, cols), BF),
            pltpu.VMEM((rows, cols), F32),
        )

    table = reduce_shapes(width, ff, devices)
    slots = len(table) * Reduce.SLOTS + 6 * Everywhere.SLOTS
    return pl.pallas_call(
        lambda *refs: backward_kernel(heads, devices, *refs),
        out_shape=shapes,
        in_specs=[anyw] * 7 + [vm] * 7 + [anyw] * 4,
        out_specs=[anyw] + [vm] * 7,
        scratch_shapes=[pltpu.VMEM(a.shape, a.dtype) for a in (norm_t, coef_t, qkv, mem, gatt, wq)] + [
            pltpu.VMEM((tokens, 3 * width), BF),
            pltpu.VMEM((brows, 512), BF),
            pltpu.VMEM((seqs, heads, 8, length), F32),
            pltpu.VMEM((3, 16, length), F32),
            pltpu.VMEM((256, length), F32),
            pltpu.VMEM((3, 2, 4, 2, 2 * width // devices, 384), BF),
            pltpu.VMEM((2, 256, width), F32),
            pltpu.VMEM((2, 256, width), BF),
            pltpu.VMEM((2, 256, width), BF),
            [buffers(i, shape) for i, shape in enumerate(table)],
            pltpu.VMEM((2, width), F32),
            pltpu.VMEM((2, 16, width), F32),
            pltpu.VMEM((10, 16, width), F32),
            pltpu.VMEM((2, 2, width), F32),
            pltpu.VMEM((10, 2, width), F32),
            pltpu.VMEM((2, 2, width), F32),
            pltpu.VMEM((10, 2, width), F32),
            pltpu.VMEM((3, 2, 8, basis), F32),
            pltpu.VMEM((3, 10, 8, basis), F32),
            pltpu.SemaphoreType.DMA((slots,)),
            pltpu.SemaphoreType.DMA((slots,)),
            pltpu.SemaphoreType.DMA((22,)),
        ],
        compiler_params=pltpu.CompilerParams(vmem_limit_bytes=56 * 1024 * 1024, collective_id=1, has_side_effects=True),
        name="backward",
    )(hidden.reshape(tokens, width), norm_t, coef_t, qkv, mem, gatt, gmid, lse, ublk, proj, wmat, vecs, vsum_a, usum, wq, p_out, g_up, g_down)


def finish_call(heads, devices, ff, early, late, msum, whole):
    width = early.shape[1]
    basis = msum.shape[1]
    e, rows = width // devices, basis // devices
    group = 4
    vm = pl.BlockSpec(memory_space=pltpu.VMEM)
    anyw = pl.BlockSpec(memory_space=pl.ANY)
    n = len(whole)

    def kernel(*refs):
        early, late, msum = refs[:3]
        sources, results = refs[3:3 + n], refs[3 + n:3 + 2 * n]
        gain_a, shift_a, qv, out_b, gain_m, shift_m, up_b, down_b, mean, wide = refs[3 + 2 * n:-1]
        sem = refs[-1]
        copies = [pltpu.make_async_copy(a, b, sem.at[i]) for i, (a, b) in enumerate(zip(sources, results))]
        for copy in copies:
            copy.start()
        me = lax.axis_index("dp") * lax.axis_size("fsdp") + lax.axis_index("fsdp")

        def thirds(x):
            high = x.astype(BF)
            rest = x - high.astype(F32)
            middle = rest.astype(BF)
            return high, middle, (rest - middle.astype(F32)).astype(BF)

        def pick(x, start, size):
            at = (iota((x.shape[1], size), 0) == iota((x.shape[1], size), 1) + start).astype(F32).astype(BF)
            return sum(dot_nn(part, at) for part in thirds(x))

        def row_of(x, i):
            return jnp.sum(jnp.where(iota(x.shape, 0) == i, x, 0.0), axis=0, keepdims=True)

        some = pick(early[0:8, :], me * e, e)
        down_b[...], gain_m[...], shift_m[...], out_b[...] = (some[i:i + 1] for i in range(4))
        some = pick(late[...], me * e, e)
        gain_a[...], shift_a[...] = some[0:1], some[1:2]
        k = devices // 2
        qv[...] = pick(row_of(late[2:4, :], me // k), me % k * 2 * e, 2 * e)
        k = devices * width // ff
        up_b[...] = pick(row_of(early[8:16, :], me // k), me % k * (ff // devices), ff // devices)
        at = (iota((rows, basis), 1) == iota((rows, basis), 0) + me * rows).astype(F32).astype(BF)
        for out, first in ((mean, 0), (wide, group)):
            x = jnp.concatenate([msum[i + first:i + first + group, :] for i in range(0, 2 * heads, 2 * group)], axis=0)
            out[...] = sum(dot_nt(at, part) for part in thirds(x))
        for copy in copies:
            copy.wait()

    small = [(1, e), (1, e), (1, 2 * e), (1, e), (1, e), (1, e), (1, ff // devices), (1, e), (rows, heads), (rows, heads)]
    return pl.pallas_call(
        kernel,
        out_shape=[jax.ShapeDtypeStruct(a.shape, a.dtype) for a in whole] + [jax.ShapeDtypeStruct(s, F32) for s in small],
        in_specs=[vm] * 3 + [anyw] * n,
        out_specs=[anyw] * n + [vm] * len(small),
        scratch_shapes=[pltpu.SemaphoreType.DMA((n,))],
        name="finish",
    )(early, late, msum, *whole)


def gather(x):
    return lax.all_gather(x, AXES, axis=0, tiled=True)


def scatter(x):
    return lax.psum_scatter(x, AXES, scatter_dimension=0, tiled=True)


def shards_plain(
    hidden, grad_out, past_states, old_coeffs, fresh_flags, ridge_map,
    gain_attn, shift_attn, qkv_weight, qv_bias, out_weight, out_bias,
    gain_mlp, shift_mlp, up_weight, up_bias, down_weight, down_bias,
    mean_weight, width_weight,
):
    seqs, length, width = hidden.shape
    heads = mean_weight.shape[1]
    devices = lax.axis_size("dp") * lax.axis_size("fsdp")
    full_qkv, full_out, full_up, full_down = (gather(w) for w in (qkv_weight, out_weight, up_weight, down_weight))
    rows = jnp.zeros((mean_weight.shape[0], 128), BF)
    rows = rows.at[:, 0:heads].set(mean_weight).at[:, 16:16 + heads].set(width_weight)
    wmat = gather(rows)
    full_qv = gather(qv_bias)
    vecs = jnp.stack(
        [gather(gain_attn), gather(shift_attn), full_qv[:width], full_qv[width:],
         gather(out_bias), gather(gain_mlp), gather(shift_mlp), gather(down_bias)]).astype(F32)
    ubias = gather(up_bias).astype(F32).reshape(-1, width)
    ubias = jnp.concatenate([ubias, jnp.zeros((8 - ubias.shape[0], width), F32)], axis=0)

    norm_t, coef_t, qkv, mem, att, lse, ublk, proj = forward_plain_call(
        heads, fresh_flags, hidden, past_states, old_coeffs, ridge_map, wmat, vecs, full_qkv)
    output, gmid, gatt, dout, dup, ddown, vsum_a, usum = middle_call(
        att, hidden, grad_out, full_out, full_up, full_down, vecs, ubias)
    gin, dqkv, vsum_b, msum = backward_plain_call(
        heads, hidden, norm_t, coef_t, qkv, mem, gatt, gmid, lse, ublk, proj, wmat, vecs, full_qkv)

    up_sum = usum.reshape(-1)[:up_bias.shape[0] * devices]
    big = [scatter(a.astype(F32)) for a in (dqkv, dout, dup, ddown)]
    small = [
        scatter(a) for a in (
            vsum_b[2], vsum_b[3], jnp.concatenate([vsum_b[0], vsum_b[1]]), vsum_a[3], vsum_a[1], vsum_a[2],
            up_sum, vsum_a[0], msum[0:heads].T, msum[16:16 + heads].T)
    ]
    return (
        output.reshape(seqs, length, width), gin.reshape(seqs, length, width),
        small[0], small[1], big[0], small[2], big[1], small[3], small[4], small[5],
        big[2], small[6], big[3], small[7], small[8], small[9],
    )


def shards_block(
    hidden, grad_out, past_states, old_coeffs, fresh_flags, ridge_map,
    gain_attn, shift_attn, qkv_weight, qv_bias, out_weight, out_bias,
    gain_mlp, shift_mlp, up_weight, up_bias, down_weight, down_bias,
    mean_weight, width_weight,
):
    seqs, length, width = hidden.shape
    heads = mean_weight.shape[1]
    devices = 32
    ff = up_weight.shape[1]
    e = width // devices
    def put(v, row, col):
        v = v.reshape((1, -1)) if v.ndim == 1 else v
        return jnp.pad(v, ((row, 32 - row - v.shape[0]), (col, 128 - col - v.shape[1])))

    small = (
        put(mean_weight, 0, 0) + put(width_weight, 0, 16)
        + put(gain_attn, 16, 0) + put(shift_attn, 16, e) + put(out_bias, 16, 2 * e) + put(gain_mlp, 16, 3 * e)
        + put(shift_mlp, 17, 0) + put(down_bias, 17, e) + put(qv_bias, 17, 2 * e) + put(up_bias, 18, 0))

    norm_t, coef_t, qkv, mem, output, gmid, gatt, dout, g_up, g_down, wq, lse, ublk, proj, wmat, vecs, vsum_a, usum = forward_call(
        heads, devices, fresh_flags, hidden, past_states, old_coeffs, ridge_map, grad_out, small, qkv_weight, out_weight, up_weight, down_weight)
    gin, d_qkv, d_out, d_up, d_down, early, late, msum = backward_call(
        heads, devices, hidden, norm_t, coef_t, qkv, mem, gatt, gmid, lse, ublk, proj, wmat, vecs, vsum_a, usum, wq,
        dout.reshape(2, 4, 2, width // 16, width), g_up, g_down, ff)

    (output, gin, d_qkv, d_out, d_up, d_down, gain_a, shift_a, qv, out_b, gain_m, shift_m, up_b, down_b, mean, wide) = finish_call(
        heads, devices, ff, early, late, msum, (output, gin, d_qkv, d_out, d_up, d_down))
    flat = lambda v: v.reshape(v.shape[1])
    return (
        output.reshape(seqs, length, width), gin.reshape(seqs, length, width),
        flat(gain_a), flat(shift_a), d_qkv, flat(qv), d_out, flat(out_b), flat(gain_m), flat(shift_m),
        d_up, flat(up_b), d_down, flat(down_b), mean, wide,
    )


def solution(mesh):
    rows = P(AXES, None)
    cube = P(AXES, None, None)
    one = P(AXES)
    in_specs = (cube, cube, cube, cube, one, P(), one, one, rows, one, rows, one, one, one, rows, one, rows, one, rows, rows)
    out_specs = (cube, cube, one, one, rows, one, rows, one, one, one, rows, one, rows, one, rows, rows)
    body = shards_block if mesh.shape["dp"] == 2 and mesh.shape["fsdp"] == 16 else shards_plain
    return jax.shard_map(body, mesh=mesh, in_specs=in_specs, out_specs=out_specs, check_vma=False)
```

time: 1210 us -> 371 us (0.31)
  waiting for transfers between devices: 642 us -> 0 us
  Pallas kernels: 0 us -> 361 us
  matrix products: 239 us -> 0 us
  blocking collectives: 160 us -> 0 us
  local copies, waits for them, and re-layouts: 84.7 us -> 0 us
  other arithmetic: 49.3 us -> 1.5 us
  between operations: 15.5 us -> 1.13 us
  loops' own time: 13.2 us -> 0 us
    reduce_scatter x4 -> x0, waiting for transfers between devices: 510 us -> none  [the longest x1 142 us: spread_grads(): lax.psum_scatter(down_weight, ('dp', 'fsdp'), scatter_dimension=0, tiled=...]
    pallas_call x0 -> x3, Pallas kernels: none -> 361 us  [the longest x1 152 us: forward_call(): pl.pallas_call(lambda *refs: forward_kernel(heads, devices, *refs), out_s...]
    dot_general x44 -> x0, matrix products: 239 us -> none  [the longest x2 20.6 us: attend_backward(): jnp.einsum('qhe,jhe->hqj', grad_att, mem_val, preferred_element_type=jnp....]
    unnamed x12 -> x0, waiting for transfers between devices: 133 us -> none
    unnamed x2 -> x0, blocking collectives: 82.3 us -> none
    all_gather x2 -> x0, blocking collectives: 77.5 us -> none  [the longest x1 40.3 us: collect(): lax.all_gather(mean_weight, ('dp', 'fsdp'), axis=0, tiled=True)]
    unnamed x162 -> x0, local copies, waits for them, and re-layouts: 28.6 us -> none
    convert_element_type x13 -> x0, other arithmetic: 25.6 us -> none  [the longest x2 14 us: attend_backward(): grad_scores = (probs * (grad_probs - inner)).astype(jnp.bfloat16)]
  transfers between devices with their start and end apart: 10 -> 0, of which waited for: 5 -> 0; matrix products, arithmetic and copies ran while one was open for 17% -> 0% of each run, Pallas kernels for 0% -> 0%
where the time goes in v1:
time: 371 us; the launch traced here: 363 us
  Pallas kernels  361 us (97%)
    pallas_call x1, Pallas kernels, forward_call(): pl.pallas_call(lambda *refs: forward_kernel(heads, devices, *refs), out_s...  152 us
    pallas_call x1, Pallas kernels, finish_call(): pl.pallas_call(kernel, out_shape=[jax.ShapeDtypeStruct(a.shape, a.dtype)...  125 us
    pallas_call x1, Pallas kernels, backward_call(): pl.pallas_call(lambda *refs: backward_kernel(heads, devices, *refs), out_...  83.6 us

profile of v1, /device:TPU:0, one launch (start us, length us, event | category | flops | bytes accessed | tf_op | source)
XLA Modules:
  0.0 363.3 jit_solution(839048176632132003)
XLA Ops:
  0.6 1.5 pad_add_fusion.refs_6_
  2.2 152.3 %forward.1 = (bf16[768,1024]{1,0:T(8,128)(2,1)}, bf16[768,1024]{1,0:T(8,128)(2,1)}, bf16[1024,2304]{1,0:T(8,128)(2,1)}, bf16[1024,1536]{1,0:T(8,128)(2,1)}, bf16...) custom-call(s32[2]{0:T(128)} %refs_0_.1, ...), custom_call_target="tpu_custom_call" | custom-call | tf_op jit(solution)/shard_map/forward/pallas_call | solution.py:1098
  154.5 83.6 %backward.1 = (bf16[1024,768]{1,0:T(8,128)(2,1)}, f32[24,2304]{1,0:T(8,128)}, f32[24,768]{1,0:T(8,128)}, f32[24,3072]{1,0:T(8,128)}, f32[96,768]{1,0:T(8,128)}, ...) custom-call(bf16[1024,768]{1,0:T(8,128)(2,1)} %bitcast.22, bf16[768,1024]{1,0:T(8,128)(2,1)} %get-tuple-element.58.refs_1_, ...), custom_call_target="tpu_custom_call" | custom-call | tf_op jit(solution)/shard_map/backward/pallas_call | solution.py:1686
  238.1 124.7 %finish.1 = (bf16[1024,768]{1,0:T(8,128)(2,1)}, bf16[1024,768]{1,0:T(8,128)(2,1)}, f32[24,2304]{1,0:T(8,128)}, f32[24,768]{1,0:T(8,128)}, f32[24,3072]{1,0:T(8,1...) custom-call(f32[16,768]{1,0:T(8,128)} %get-tuple-element.75.refs_0_,, ...), custom_call_target="tpu_custom_call" | custom-call | tf_op jit(solution)/shard_map/finish/pallas_call | solution.py:1768

commit v2 on v1

--- a/solution.py
+++ b/solution.py
@@ -578,8 +578,6 @@
             return 0
 
         lax.fori_loop(0, 4, step, 0)
-        for copy in self.down_third(t):
-            copy.start()
 
     def down_add_third(self, t):
         p, h = self.p, self.h
@@ -627,7 +625,8 @@
             return 0
 
         lax.fori_loop(0, 16, step, 0)
-        self.up_second(i).start()
+        if i < 2:
+            self.up_second(i).start()
 
     def up_add_second(self, i):
         p = self.p
@@ -649,10 +648,16 @@
             self.down_core(i).wait_send()
             self.up_core(i).wait_send()
         for t in (0, 1):
-            for copy in self.down_second(t) + self.down_third(t):
+            for copy in self.down_second(t):
                 copy.wait_send()
-        for i in range(4):
-            self.up_second(i).wait_send()
+            self.up_second(t).wait_send()
+
+    def resume(self):
+        for copy in self.resumed():
+            copy.start()
+
+    def resumed(self):
+        return [self.up_second(2), self.up_second(3), *self.down_third(0), *self.down_third(1)]
 
 
 def forward_coeffs(s, flags, past, old, ridge, coeffs, coef_t):
@@ -902,20 +907,17 @@
         elif where == "second":
             er.up_core(i).start()
             at(0, (er.down_add_core, 0))
-            at(1, (er.down_add_second, 0))
+            at(2, (er.down_add_second, 0))
         elif where == "middle":
             at(2, (er.down_add_core, 1))
-            at(3, (er.up_add_core, 2), (er.down_add_third, 0))
         elif where == "both":
             at(0, (er.up_add_core, 0))
             at(1, (er.up_add_core, 1))
         elif where == "leave":
-            at(0, (er.up_add_core, 3), (er.down_add_second, 1))
+            at(0, (er.up_add_core, 2), (er.up_add_core, 3))
             at(2, (er.up_add_second, 0), (er.up_add_second, 1))
         elif where == "end":
-            er.up_add_second(2)
-            er.down_add_third(1)
-            er.up_add_second(3)
+            er.down_add_second(1)
 
     wflat = wq.reshape(width, 3 * width)
 
@@ -923,8 +925,7 @@
         middle_body(
             att, hidden, gout, wo.reshape(width, width), wu.reshape(width, ff), wd.reshape(ff, width), vecs, ubias, vsum, usum,
             wflat.at[:, 0:tokens], wflat.at[:, tokens:tokens + width], *scratch, (output_h, gmid_h, gatt_h, dout_h), local, sem, er.put_down, er.put_up, hook)
-        out = [pltpu.make_async_copy(er.g_u, gu_h, local.at[sem + 14])] + [
-            pltpu.make_async_copy(er.g_d.at[t, p.y, :, p.x], gd_h.at[2 * t:2 * t + 2], local.at[sem + 15 + t]) for t in (0, 1)]
+        out = [pltpu.make_async_copy(er.g_u, gu_h, local.at[sem + 14]), pltpu.make_async_copy(er.g_d, gd_h, local.at[sem + 15])]
         for copy in out:
             copy.start()
         er.left()
@@ -1089,7 +1090,7 @@
     far = [
         ((width, tokens), BF), ((width, seqs * basis), BF), ((tokens, 3 * width), BF), ((seqs * basis, 2 * width), BF),
         ((tokens, width), BF), ((tokens, width), F32), ((tokens, width), BF),
-        ((width, width), BF), ((2, 2, 4, 2, chip, 2 * n), BF), ((4, chip_ff, n), BF), (full, BF)]
+        ((width, width), BF), ((2, 2, 4, 2, chip, 2 * n), BF), ((2, 2, 2, 2, chip_ff, n), BF), (full, BF)]
     near = [
         ((seqs, heads, 1, length), F32), ((seqs, 32, width), F32), ((seqs, 32, length), F32),
         ((basis, 128), BF), ((8, width), F32), ((8, width), F32), ((8, width), F32)]
@@ -1117,7 +1118,7 @@
             [pltpu.VMEM(shape, BF) for shape in (
                 (2, 2, 2, 2, chip_ff, n), (2, 2, 4, 2, chip, 2 * n), (2, 2, 2, chip_ff, n), (2, 2, 4, 2, chip, n),
                 (2, 2, 2, 2, chip_ff, n), (4, 2, 4, 2, chip, n),
-                (2, 2, 2, 2, chip_ff // 2, n), (2, 4, 2, chip, n), (2, 2, 4, chip, n), (2, 2, 2, chip_ff // 2, n))],
+                (2, 2, 2, 2, chip_ff // 2, n), (2, 4, 2, chip, n), (2, 2, 4, chip, n), (8, 128))],
             pltpu.SemaphoreType.DMA((slots,)),
             pltpu.SemaphoreType.DMA((slots,)),
             pltpu.SemaphoreType.DMA((9 + 2 * seqs + 3 + 17,)),
@@ -1412,9 +1413,11 @@
         lax.fori_loop(0, 4, step, 0)
         self.send_along()
 
+    early = None
+
     def summand(self, z):
         p = self.p
-        return self.g.at[z] if len(self.g.shape) == 3 else self.g.at[p.y, z, p.x]
+        return self.g.at[p.y, z, p.x] if self.early is None else self.early.at[z // 2, p.y, z % 2, p.x]
 
     def send_along(self):
         p = self.p
@@ -1467,11 +1470,11 @@
 
 
 BACK_STEPS = (
-    (), (), ("a3", "b3", "o1"), ("e0",),
-    ("u0", "o2"), ("p1", "d4"), ("e1", "p2"), ("u1", "o3", "a4"),
-    ("q1",), ("p3", "b4", "v0"), ("q2",), ("p4", "o4"),
-    ("r1", "v1"), ("k0", "w0", "q3"), (), ("r2", "w1", "k1"),
-    ("l0",), ("r3",), ("l1",), ("q4",), ("r4",),
+    (), (), (), ("xx", "o1"),
+    (), ("p1",), ("a3", "b3", "e0"), ("o2", "u0"),
+    (), ("q1", "p2", "e1"), ("o3", "u1"), (),
+    ("p3", "r1", "v0"), ("q2",), (), ("w0", "k0"),
+    ("r2", "v1", "q3"), ("l0",), ("r3", "w1", "k1"), ("l1", "d4", "a4", "b4", "p4", "o4", "q4"), ("r4",),
 )
 
 
@@ -1481,7 +1484,7 @@
     gin, o_qkv, o_out, o_up, o_down, early, late, msum,
     norm_t, coef_t, qkv, mem, gatt, wq,
     gqkv, gmem, head_par, grows, dq_t, away, gm_buf, hid_buf, gin_buf,
-    bufs, vsum, e_held, e_got, l_held, l_got, k_held, k_got, m_held, m_got, send, recv, local,
+    bufs, vsum, e_held, e_got, l_held, l_got, k_held, k_got, m_held, m_got, early_bufs, send, recv, local, early_send, early_recv,
 ):
     place = Place()
     p = place
@@ -1504,14 +1507,16 @@
         loads.append(copy)
     grows[...] = jnp.zeros_like(grows)
     vsum[...] = jnp.zeros_like(vsum)
-    e_held[0] = jnp.concatenate([vsum_a[...], usum[...]], axis=0)
+    e_held[0] = jnp.concatenate([vsum_a[0:4, :], usum[0:4, :]], axis=0)
     half = width // 2
 
     def side(c):
         return p_out.at[:, :, :, :, pl.ds(pl.multiple_of(c * half, 128), half)]
 
-    own = [pltpu.make_async_copy(src, red[n].g, local.at[6 + i])
-           for i, (n, src) in enumerate((("a", gu_h.at[0]), ("b", gu_h.at[1]), ("d", gd_h), ("o", side(p.c))))]
+    er = EarlyReduce(place, early_send, early_recv, *early_bufs[:2], None, None, None, None, None, *early_bufs[2:])
+    red["a"].g, red["b"].g, red["d"].early = er.g_u.at[0], er.g_u.at[1], er.g_d
+    own = [pltpu.make_async_copy(src, dst, local.at[6 + i])
+           for i, (src, dst) in enumerate(((gu_h, er.g_u), (gd_h, er.g_d), (side(p.c), red["o"].g)))]
     for copy in own:
         copy.start()
     place.greet(place.layer())
@@ -1519,9 +1524,7 @@
     sums["e"].start(0)
     for copy in own:
         copy.wait()
-    red["d"].send_along()
-    red["a"].send_third(0)
-    red["b"].send_third(1)
+    er.resume()
     pieces = 128
     outs = {
         "a": (o_up, lambda: [(k * half, k * width + p.c * half, half) for k in (0, 1)]),
@@ -1533,7 +1536,15 @@
         outs[n] = (o_qkv, lambda i=i: [(j * pieces, j * width + i * 2 * pieces + p.c * pieces, pieces) for j in range(3)])
 
     def perform(word):
-        if word[0] in sums:
+        if word[0] == "x":
+            er.up_add_second(2)
+            er.up_add_second(3)
+            red["a"].send_third(0)
+            red["b"].send_third(1)
+            er.down_add_third(0)
+            er.down_add_third(1)
+            red["d"].send_along()
+        elif word[0] in sums:
             total, step = sums[word[0]], int(word[1])
             value = total.add(step)
             if step == 0:
@@ -1635,6 +1646,8 @@
         red[n].done()
     for i in (blocks - 2, blocks - 1):
         emit(i).wait()
+    for copy in er.resumed():
+        copy.wait_send()
     st.left()
 
 
@@ -1661,7 +1674,7 @@
         jax.ShapeDtypeStruct((width // devices, width), F32),
         jax.ShapeDtypeStruct((width // devices, ff), F32),
         jax.ShapeDtypeStruct((ff // devices, width), F32),
-        jax.ShapeDtypeStruct((16, width), F32),
+        jax.ShapeDtypeStruct((8, width), F32),
         jax.ShapeDtypeStruct((4, width), F32),
         jax.ShapeDtypeStruct((24, basis), F32),
     )
@@ -1673,7 +1686,7 @@
         sizes = [parts.get(k, (0, 16, 0, 128)) for k in (0, 1)]
         (_, ra, _, ca), (_, rb, _, cb) = sizes
         return (
-            pltpu.VMEM((4, rows, cols) if i == 2 else (2, 4, 2, rows, cols), BF),
+            none if i < 3 else pltpu.VMEM((2, 4, 2, rows, cols), BF),
             pltpu.VMEM((2, 4, 2, rows, cols), BF) if whole else none,
             (pltpu.VMEM((4, 2, ra, ca), BF), pltpu.VMEM((2, 4, rb, cb), BF)) if whole else (none, none),
             (pltpu.VMEM((4, ra, ca), BF), pltpu.VMEM((4, rb, cb), BF)),
@@ -1681,6 +1694,7 @@
             pltpu.VMEM((rows, cols), F32),
         )
 
+    chip, chip_ff = 2 * width // devices, 2 * ff // devices
     table = reduce_shapes(width, ff, devices)
     slots = len(table) * Reduce.SLOTS + 6 * Everywhere.SLOTS
     return pl.pallas_call(
@@ -1700,17 +1714,21 @@
             pltpu.VMEM((2, 256, width), BF),
             [buffers(i, shape) for i, shape in enumerate(table)],
             pltpu.VMEM((2, width), F32),
-            pltpu.VMEM((2, 16, width), F32),
-            pltpu.VMEM((10, 16, width), F32),
+            pltpu.VMEM((2, 8, width), F32),
+            pltpu.VMEM((10, 8, width), F32),
             pltpu.VMEM((2, 2, width), F32),
             pltpu.VMEM((10, 2, width), F32),
             pltpu.VMEM((2, 2, width), F32),
             pltpu.VMEM((10, 2, width), F32),
             pltpu.VMEM((3, 2, 8, basis), F32),
             pltpu.VMEM((3, 10, 8, basis), F32),
+            [pltpu.VMEM(shape, BF) for shape in (
+                g_down.shape, g_up.shape, (2, 4, 2, chip, width // 2), (2, 2, 4, chip, width // 2), (2, 2, 2, chip_ff // 2, width // 2))],
             pltpu.SemaphoreType.DMA((slots,)),
             pltpu.SemaphoreType.DMA((slots,)),
             pltpu.SemaphoreType.DMA((22,)),
+            pltpu.SemaphoreType.DMA((EarlyReduce.SLOTS,)),
+            pltpu.SemaphoreType.DMA((EarlyReduce.SLOTS,)),
         ],
         compiler_params=pltpu.CompilerParams(vmem_limit_bytes=56 * 1024 * 1024, collective_id=1, has_side_effects=True),
         name="backward",
@@ -1749,14 +1767,14 @@
         def row_of(x, i):
             return jnp.sum(jnp.where(iota(x.shape, 0) == i, x, 0.0), axis=0, keepdims=True)
 
-        some = pick(early[0:8, :], me * e, e)
+        some = pick(early[...], me * e, e)
         down_b[...], gain_m[...], shift_m[...], out_b[...] = (some[i:i + 1] for i in range(4))
         some = pick(late[...], me * e, e)
         gain_a[...], shift_a[...] = some[0:1], some[1:2]
         k = devices // 2
         qv[...] = pick(row_of(late[2:4, :], me // k), me % k * 2 * e, 2 * e)
         k = devices * width // ff
-        up_b[...] = pick(row_of(early[8:16, :], me // k), me % k * (ff // devices), ff // devices)
+        up_b[...] = pick(row_of(early[4:8, :], me // k), me % k * (ff // devices), ff // devices)
         at = (iota((rows, basis), 1) == iota((rows, basis), 0) + me * rows).astype(F32).astype(BF)
         for out, first in ((mean, 0), (wide, group)):
             x = jnp.concatenate([msum[i + first:i + first + group, :] for i in range(0, 2 * heads, 2 * group)], axis=0)
@@ -1768,7 +1786,7 @@
     return pl.pallas_call(
         kernel,
         out_shape=[jax.ShapeDtypeStruct(a.shape, a.dtype) for a in whole] + [jax.ShapeDtypeStruct(s, F32) for s in small],
-        in_specs=[vm] * 3 + [anyw] * n,
+        in_specs=[vm] * (3 + n),
         out_specs=[anyw] * n + [vm] * len(small),
         scratch_shapes=[pltpu.SemaphoreType.DMA((n,))],
         name="finish",

time: 371 us -> 240 us (0.65); the launches traced: 363 us -> 236 us
  Pallas kernels: 361 us -> 234 us
    pallas_call x1, Pallas kernels: 125 us -> 4.79 us  [finish_call(): pl.pallas_call(kernel, out_shape=[jax.ShapeDtypeStruct(a.shape, a.dtype)...]
    pallas_call x1, Pallas kernels: 152 us -> 145 us  [forward_call(): pl.pallas_call(lambda *refs: forward_kernel(heads, devices, *refs), out_s...]
where the time goes in v2:
time: 240 us; the launch traced here: 236 us
  Pallas kernels  234 us (98%)
    pallas_call x1, Pallas kernels, forward_call(): pl.pallas_call(lambda *refs: forward_kernel(heads, devices, *refs), out_s...  145 us
    pallas_call x1, Pallas kernels, backward_call(): pl.pallas_call(lambda *refs: backward_kernel(heads, devices, *refs), out_...  83.5 us

profile of v2, /device:TPU:0, one launch (start us, length us, event | category | flops | bytes accessed | tf_op | source)
XLA Modules:
  0.0 236.1 jit_solution(10976345746529136215)
XLA Ops:
  0.6 1.5 pad_add_fusion.refs_6_
  2.2 145.4 %forward.1 = (bf16[768,1024]{1,0:T(8,128)(2,1)}, bf16[768,1024]{1,0:T(8,128)(2,1)}, bf16[1024,2304]{1,0:T(8,128)(2,1)}, bf16[1024,1536]{1,0:T(8,128)(2,1)}, bf16...) custom-call(s32[2]{0:T(128)} %refs_0_.1, ...), custom_call_target="tpu_custom_call" | custom-call | tf_op jit(solution)/shard_map/forward/pallas_call | solution.py:1099
  147.6 83.5 %backward.1 = (bf16[1024,768]{1,0:T(8,128)(2,1)}, f32[24,2304]{1,0:T(8,128)}, f32[24,768]{1,0:T(8,128)}, f32[24,3072]{1,0:T(8,128)}, f32[96,768]{1,0:T(8,128)}, ...) custom-call(bf16[1024,768]{1,0:T(8,128)(2,1)} %bitcast.22, bf16[768,1024]{1,0:T(8,128)(2,1)} %get-tuple-element.58.refs_1_, ...), custom_call_target="tpu_custom_call" | custom-call | tf_op jit(solution)/shard_map/backward/pallas_call | solution.py:1700
  231.1 4.8 %finish.1 = (bf16[1024,768]{1,0:T(8,128)(2,1)}, bf16[1024,768]{1,0:T(8,128)(2,1)}, f32[24,2304]{1,0:T(8,128)}, f32[24,768]{1,0:T(8,128)}, f32[24,3072]{1,0:T(8,1...) custom-call(f32[8,768]{1,0:T(8,128)} %get-tuple-element.75.refs_0_, ...), custom_call_target="tpu_custom_call" | custom-call | tf_op jit(solution)/shard_map/finish/pallas_call | solution.py:1786

commit v3 on v2

--- a/solution.py
+++ b/solution.py
@@ -75,14 +75,15 @@
             self.at(z=self.far_z(s)) for s in (1, 2, 3)]
 
     def layer(self):
-        return [self.at(y=(self.y + d // 4) % 2, x=(self.x + d // 2) % 2, c=(self.c + d) % 2) for d in range(1, 8)] + [
-            self.at(z=self.far_z(s)) for s in (1, 2, 3)]
-
-    def greet(self, devices):
+        return self.others() + [self.at(y=1 - self.y, x=1 - self.x)]
+
+    def hello(self, devices):
         barrier = pltpu.get_barrier_semaphore()
         for d in devices:
             pl.semaphore_signal(barrier, inc=1, device_id=d, device_id_type=MESH)
-        pl.semaphore_wait(barrier, len(devices))
+
+    def wait_hello(self, devices):
+        pl.semaphore_wait(pltpu.get_barrier_semaphore(), len(devices))
 
 
 class Weight:
@@ -724,6 +725,12 @@
     return centre, wide, variance, root
 
 
+def causal(scores, allowed):
+    n = allowed.shape[0]
+    last = jnp.where(allowed, scores[-n:], -1e30)
+    return last if scores.shape[0] == n else jnp.concatenate([scores[:-n], last], axis=0)
+
+
 def forward_heads(s, first, last, heads, length, basis, width, qkv, mem, att, lse, head_par, att_t):
     hd = width // heads
     half = length // 2
@@ -739,6 +746,7 @@
         v_t = qkv[rows, pl.ds(pl.multiple_of(2 * width + c0, 2 * hd), 2 * hd)].T
         mv_t = mem[brows, pl.ds(pl.multiple_of(width + c0, 2 * hd), 2 * hd)].T
         cent = ((iota((basis, 1), 0).astype(F32) + 0.5) / basis)
+        allowed = iota((half, half), 0) <= iota((half, half), 1)
         for h in range(2):
             head = p * 2 + h
             km = k * masks[h]
@@ -746,9 +754,7 @@
             for b in range(2):
                 cols = slice(b * half, (b + 1) * half)
                 depth = (b + 1) * half
-                sc = dot_nt(km[:depth], q[cols]) * scale
-                allowed = iota((depth, half), 0) <= iota((depth, half), 1) + b * half
-                sc = jnp.where(allowed, sc, -1e30)
+                sc = causal(dot_nt(km[:depth], q[cols]) * scale, allowed)
                 top = jnp.max(sc, axis=0, keepdims=True)
                 e = jnp.exp2(sc - top)
                 total = jnp.sum(e, axis=0, keepdims=True)
@@ -952,6 +958,7 @@
     seqs, length = past.shape[0], past.shape[1]
     basis = ridge.shape[0]
     ff = up_s.shape[1]
+    place.hello(place.others())
     loads = []
     for i, (src, dst) in enumerate(((ridge_h, ridge), (old_h, old), (past_h, past), (hidden_h, hidden), (gout_h, gout))):
         copy = pltpu.make_async_copy(src, dst, local.at[i])
@@ -968,7 +975,7 @@
     hd_cols = width // 2
     block_d[pl.ds(pl.multiple_of(p.c * ed, 16), ed), :] = down_s[:, pl.ds(pl.multiple_of(p.c * hd_cols, 128), hd_cols)]
 
-    place.greet(place.others())
+    place.wait_hello(place.others())
     mate = p.at(c=1 - p.c)
     there = pl.multiple_of((1 - p.c) * nh, 128)
     st.go("wide", wide_s.at[:, pl.ds(there, t_qkv.half)], wide_r.at[:, 0:t_qkv.half], base, mate)
@@ -1191,6 +1198,7 @@
     ga = gatt[rows, pl.ds(c0, 2 * hd)]
     k_t = k.T
     cent = ((iota((basis, 1), 0).astype(F32) + 0.5) / basis)
+    allowed = iota((half, half), 0) <= iota((half, half), 1)
     dv = [0.0, 0.0]
     dk = [0.0, 0.0]
     dmv = 0.0
@@ -1201,10 +1209,8 @@
         for b in range(2):
             cols = slice(b * half, (b + 1) * half)
             depth = (b + 1) * half
-            sc = dot_nt(km[:depth], q[cols]) * scale
-            pr = jnp.exp2(sc - lse[s, head, :, cols])
-            allowed = iota((depth, half), 0) <= iota((depth, half), 1) + b * half
-            pr = jnp.where(allowed, pr, 0.0)
+            sc = dot_nt(km[:depth], q[cols]) * scale - lse[s, head, :, cols]
+            pr = jnp.exp2(causal(sc, allowed))
             dp = dot_nt(vm[:depth], ga[cols])
             inner = jnp.sum(pr * dp, axis=0, keepdims=True)
             ds = (pr * (dp - inner)).astype(BF)
@@ -1443,38 +1449,49 @@
 
 
 class Everywhere:
-    SLOTS = 10
+    SLOTS = 8
 
     def __init__(self, place, started, name, slot, held, got):
         self.p, self.s, self.name, self.slot, self.held, self.got = place, started, name, slot, held, got
+        n = held.shape[-1] // 2
+        self.half = pl.ds(pl.multiple_of(place.c * n, 128), n)
 
     def start(self, step):
-        p = self.p
+        p, name, half = self.p, (self.name, step), self.half
         if step == 0:
-            for d in range(1, 8):
-                to = p.at(y=(p.y + d // 4) % 2, x=(p.x + d // 2) % 2, c=(p.c + d) % 2)
-                self.s.go((self.name, 0), self.held.at[0], self.got.at[d - 1], self.slot + d - 1, to)
+            self.s.go(name, self.held.at[0], self.got.at[0], self.slot, p.at(c=1 - p.c))
+        elif step == 1:
+            for d in (1, 2, 3):
+                to = p.at(y=(p.y + d // 2) % 2, x=(p.x + d) % 2)
+                self.s.go(name, self.held.at[1, :, half], self.got.at[d, :, half], self.slot + d, to)
+        elif step == 2:
+            for s in (1, 2, 3):
+                self.s.go(name, self.held.at[2, :, half], self.got.at[3 + s, :, half], self.slot + 3 + s, p.at(z=p.far_z(s)))
         else:
-            for s in (1, 2, 3):
-                self.s.go((self.name, 1), self.held.at[1], self.got.at[6 + s], self.slot + 6 + s, p.at(z=p.far_z(s)))
+            ref = self.held.at[3, :, half]
+            self.s.go(name, ref, ref, self.slot + 7, p.at(c=1 - p.c))
 
     def add(self, step):
         self.s.arrived((self.name, step))
-        first = 0 if step == 0 else 7
-        total = self.held[step]
-        for i in range(first, 7 if step == 0 else 10):
-            total = total + self.got[i]
+        half = self.half
         if step == 0:
-            self.held[1] = total
-        return total
+            self.held[1] = self.held[0] + self.got[0]
+        elif step < 3:
+            i = 1 if step == 1 else 4
+            self.held[step + 1, :, half] = (self.held[step, :, half] + self.got[i, :, half]) + (
+                self.got[i + 1, :, half] + self.got[i + 2, :, half])
+        else:
+            return self.held[3]
+        self.start(step + 1)
+        return None
 
 
 BACK_STEPS = (
-    (), (), (), ("xx", "o1"),
-    (), ("p1",), ("a3", "b3", "e0"), ("o2", "u0"),
-    (), ("q1", "p2", "e1"), ("o3", "u1"), (),
-    ("p3", "r1", "v0"), ("q2",), (), ("w0", "k0"),
-    ("r2", "v1", "q3"), ("l0",), ("r3", "w1", "k1"), ("l1", "d4", "a4", "b4", "p4", "o4", "q4"), ("r4",),
+    (), (), (), (),
+    ("xx", "o1"), ("p1",), ("a3", "b3"), ("o2",),
+    ("q1",), ("p2",), ("o3",), ("p3", "q2"),
+    ("r1",), ("q3",), ("w0", "k0"), ("r2", "w1", "k1"),
+    ("l0",), ("r3", "l1", "w2", "k2"), ("l2", "w3", "k3", "d4", "a4", "b4", "p4", "o4", "q4"), ("l3", "r4"),
 )
 
 
@@ -1484,7 +1501,7 @@
     gin, o_qkv, o_out, o_up, o_down, early, late, msum,
     norm_t, coef_t, qkv, mem, gatt, wq,
     gqkv, gmem, head_par, grows, dq_t, away, gm_buf, hid_buf, gin_buf,
-    bufs, vsum, e_held, e_got, l_held, l_got, k_held, k_got, m_held, m_got, early_bufs, send, recv, local, early_send, early_recv,
+    bufs, vsum, k_held, k_got, l_held, l_got, m_held, m_got, early_bufs, send, recv, local, early_send, early_recv,
 ):
     place = Place()
     p = place
@@ -1496,10 +1513,8 @@
     names = "abdopqr"
     red = {n: Reduce(place, st, n, i * Reduce.SLOTS, parts, bufs[i]) for i, (n, (_, _, parts)) in enumerate(zip(names, reduce_shapes(width, ff, devices)))}
     base = len(names) * Reduce.SLOTS
-    sums = {"e": Everywhere(place, st, "e", base, e_held, e_got), "l": Everywhere(place, st, "l", base + Everywhere.SLOTS, l_held, l_got)}
-    sums["k"] = Everywhere(place, st, "k", base + 5 * Everywhere.SLOTS, k_held, k_got)
-    for i, n in enumerate("uvw"):
-        sums[n] = Everywhere(place, st, n, base + (2 + i) * Everywhere.SLOTS, m_held.at[i], m_got.at[i])
+    sums = {n: Everywhere(place, st, n, base + i * Everywhere.SLOTS, held, got)
+            for i, (n, held, got) in enumerate((("k", k_held, k_got), ("w", m_held, m_got), ("l", l_held, l_got)))}
     loads = []
     for i, (src, dst) in enumerate(((qkv_h, qkv), (mem_h, mem), (gatt_h, gatt), (norm_h, norm_t), (coef_h, coef_t), (wq_h, wq))):
         copy = pltpu.make_async_copy(src, dst, local.at[i])
@@ -1507,7 +1522,7 @@
         loads.append(copy)
     grows[...] = jnp.zeros_like(grows)
     vsum[...] = jnp.zeros_like(vsum)
-    e_held[0] = jnp.concatenate([vsum_a[0:4, :], usum[0:4, :]], axis=0)
+    k_held[0] = jnp.concatenate([vsum_a[0:4, :], usum[0:4, :], jnp.zeros((8, width), F32)], axis=0)
     half = width // 2
 
     def side(c):
@@ -1519,12 +1534,14 @@
            for i, (src, dst) in enumerate(((gu_h, er.g_u), (gd_h, er.g_d), (side(p.c), red["o"].g)))]
     for copy in own:
         copy.start()
-    place.greet(place.layer())
-    red["o"].core((side(1 - p.c), slice(None)))
-    sums["e"].start(0)
-    for copy in own:
-        copy.wait()
-    er.resume()
+    place.hello(place.layer())
+
+    def begin():
+        place.wait_hello(place.layer())
+        red["o"].core((side(1 - p.c), slice(None)))
+        for copy in own:
+            copy.wait()
+        er.resume()
     pieces = 128
     outs = {
         "a": (o_up, lambda: [(k * half, k * width + p.c * half, half) for k in (0, 1)]),
@@ -1547,14 +1564,14 @@
         elif word[0] in sums:
             total, step = sums[word[0]], int(word[1])
             value = total.add(step)
-            if step == 0:
-                total.start(1)
-            else:
-                if word[0] in "uvw":
-                    n = value.shape[0]
-                    msum["uvw".index(word[0]) * n:("uvw".index(word[0]) + 1) * n, :] = value
+            if step == 3:
+                if word[0] == "w":
+                    msum[...] = value
+                elif word[0] == "l":
+                    late[0:2, :] = value
                 else:
-                    {"e": early, "l": late.at[0:2, :], "k": late.at[2:4, :]}[word[0]][...] = value
+                    early[...] = value[0:8]
+                    late[2:4, :] = value[8:10]
         else:
             r, step = red[word[0]], word[1]
             if step == "1":
@@ -1586,9 +1603,11 @@
                     return 0
 
                 lax.fori_loop(2 * i + k, 2 * i + k + 1, one, 0)
+                if i + s + k == 0:
+                    begin()
                 if k == 0:
                     advance()
-            backward_finish(s, i * chunk, heads, rows_of[s], qkv, mem, ublk, grows, dq_t, wmat, gqkv, gmem, m_held.at[i, 0])
+            backward_finish(s, i * chunk, heads, rows_of[s], qkv, mem, ublk, grows, dq_t, wmat, gqkv, gmem, m_held.at[0, 8 * i:8 * i + 8, :])
             if s < seqs - 1:
                 advance()
         if i == 0:
@@ -1606,9 +1625,9 @@
             r.g[:, :, :, :, j * pieces:(j + 1) * pieces] = keep
             away[i, :, :, :, :, j * pieces:(j + 1) * pieces] = give
         r.core((away.at[i], slice(None)))
-        sums["uvw"[i]].start(0)
         if i == 2:
-            bias_sums(width, gqkv, k_held.at[0])
+            sums["w"].start(0)
+            bias_sums(width, gqkv, k_held.at[0, 8:10, :])
             sums["k"].start(0)
         advance()
     wflat = wq.reshape(width, 3 * width)
@@ -1696,7 +1715,7 @@
 
     chip, chip_ff = 2 * width // devices, 2 * ff // devices
     table = reduce_shapes(width, ff, devices)
-    slots = len(table) * Reduce.SLOTS + 6 * Everywhere.SLOTS
+    slots = len(table) * Reduce.SLOTS + 3 * Everywhere.SLOTS
     return pl.pallas_call(
         lambda *refs: backward_kernel(heads, devices, *refs),
         out_shape=shapes,
@@ -1714,14 +1733,12 @@
             pltpu.VMEM((2, 256, width), BF),
             [buffers(i, shape) for i, shape in enumerate(table)],
             pltpu.VMEM((2, width), F32),
-            pltpu.VMEM((2, 8, width), F32),
-            pltpu.VMEM((10, 8, width), F32),
-            pltpu.VMEM((2, 2, width), F32),
-            pltpu.VMEM((10, 2, width), F32),
-            pltpu.VMEM((2, 2, width), F32),
-            pltpu.VMEM((10, 2, width), F32),
-            pltpu.VMEM((3, 2, 8, basis), F32),
-            pltpu.VMEM((3, 10, 8, basis), F32),
+            pltpu.VMEM((4, 16, width), F32),
+            pltpu.VMEM((7, 16, width), F32),
+            pltpu.VMEM((4, 2, width), F32),
+            pltpu.VMEM((7, 2, width), F32),
+            pltpu.VMEM((4, 24, basis), F32),
+            pltpu.VMEM((7, 24, basis), F32),
             [pltpu.VMEM(shape, BF) for shape in (
                 g_down.shape, g_up.shape, (2, 4, 2, chip, width // 2), (2, 2, 4, chip, width // 2), (2, 2, 2, chip_ff // 2, width // 2))],
             pltpu.SemaphoreType.DMA((slots,)),

time: 240 us -> 233 us (0.971)
  Pallas kernels: 234 us -> 228 us
    pallas_call x1, Pallas kernels: 83.5 us -> 78 us  [backward_call(): pl.pallas_call(lambda *refs: backward_kernel(heads, devices, *refs), out_...]
where the time goes in v3:
time: 233 us; the launch traced here: 231 us
  Pallas kernels  228 us (98%)
    pallas_call x1, Pallas kernels, forward_call(): pl.pallas_call(lambda *refs: forward_kernel(heads, devices, *refs), out_s...  145 us
    pallas_call x1, Pallas kernels, backward_call(): pl.pallas_call(lambda *refs: backward_kernel(heads, devices, *refs), out_...  78 us
    pallas_call x1, Pallas kernels, finish_call(): pl.pallas_call(kernel, out_shape=[jax.ShapeDtypeStruct(a.shape, a.dtype)...  4.79 us

profile of v3, /device:TPU:0, one launch (start us, length us, event | category | flops | bytes accessed | tf_op | source)
XLA Modules:
  0.0 230.6 jit_solution(7440575705827208667)
XLA Ops:
  0.6 1.5 pad_add_fusion.refs_6_
  2.2 145.3 %forward.1 = (bf16[768,1024]{1,0:T(8,128)(2,1)}, bf16[768,1024]{1,0:T(8,128)(2,1)}, bf16[1024,2304]{1,0:T(8,128)(2,1)}, bf16[1024,1536]{1,0:T(8,128)(2,1)}, bf16...) custom-call(s32[2]{0:T(128)} %refs_0_.1, ...), custom_call_target="tpu_custom_call" | custom-call | tf_op jit(solution)/shard_map/forward/pallas_call | solution.py:1106
  147.5 78.0 %backward.1 = (bf16[1024,768]{1,0:T(8,128)(2,1)}, f32[24,2304]{1,0:T(8,128)}, f32[24,768]{1,0:T(8,128)}, f32[24,3072]{1,0:T(8,128)}, f32[96,768]{1,0:T(8,128)}, ...) custom-call(bf16[1024,768]{1,0:T(8,128)(2,1)} %bitcast.22, bf16[768,1024]{1,0:T(8,128)(2,1)} %get-tuple-element.58.refs_1_, ...), custom_call_target="tpu_custom_call" | custom-call | tf_op jit(solution)/shard_map/backward/pallas_call | solution.py:1719
  225.5 4.8 %finish.1 = (bf16[1024,768]{1,0:T(8,128)(2,1)}, bf16[1024,768]{1,0:T(8,128)(2,1)}, f32[24,2304]{1,0:T(8,128)}, f32[24,768]{1,0:T(8,128)}, f32[24,3072]{1,0:T(8,1...) custom-call(f32[8,768]{1,0:T(8,128)} %get-tuple-element.75.refs_0_, ...), custom_call_target="tpu_custom_call" | custom-call | tf_op jit(solution)/shard_map/finish/pallas_call | solution.py:1803

commit v4 on v3

--- a/solution.py
+++ b/solution.py
@@ -912,16 +912,16 @@
                 pass_on(word)
         elif where == "second":
             er.up_core(i).start()
-            at(0, (er.down_add_core, 0))
-            at(2, (er.down_add_second, 0))
+            at(1, (er.down_add_core, 0))
+            at(3, (er.down_add_second, 0))
         elif where == "middle":
             at(2, (er.down_add_core, 1))
         elif where == "both":
             at(0, (er.up_add_core, 0))
             at(1, (er.up_add_core, 1))
         elif where == "leave":
-            at(0, (er.up_add_core, 2), (er.up_add_core, 3))
-            at(2, (er.up_add_second, 0), (er.up_add_second, 1))
+            at(1, (er.up_add_core, 2), (er.up_add_core, 3))
+            at(3, (er.up_add_second, 0), (er.up_add_second, 1))
         elif where == "end":
             er.down_add_second(1)
 
@@ -1487,9 +1487,9 @@
 
 
 BACK_STEPS = (
-    (), (), (), (),
-    ("xx", "o1"), ("p1",), ("a3", "b3"), ("o2",),
-    ("q1",), ("p2",), ("o3",), ("p3", "q2"),
+    (), (), (), (), (),
+    ("xx", "o1"), ("p1",), ("a3", "b3"), ("o2", "q1"),
+    ("p2",), ("o3", "q2"), ("p3",),
     ("r1",), ("q3",), ("w0", "k0"), ("r2", "w1", "k1"),
     ("l0",), ("r3", "l1", "w2", "k2"), ("l2", "w3", "k3", "d4", "a4", "b4", "p4", "o4", "q4"), ("l3", "r4"),
 )
@@ -1764,10 +1764,11 @@
     def kernel(*refs):
         early, late, msum = refs[:3]
         sources, results = refs[3:3 + n], refs[3 + n:3 + 2 * n]
-        gain_a, shift_a, qv, out_b, gain_m, shift_m, up_b, down_b, mean, wide = refs[3 + 2 * n:-1]
-        sem = refs[-1]
-        copies = [pltpu.make_async_copy(a, b, sem.at[i]) for i, (a, b) in enumerate(zip(sources, results))]
-        for copy in copies:
+        gain_a, shift_a, qv, out_b, gain_m, shift_m, up_b, down_b, mean, wide = refs[3 + 2 * n:-1 - n]
+        held, sem = refs[-1 - n:-1], refs[-1]
+        taken = [pltpu.make_async_copy(a, b, sem.at[i]) for i, (a, b) in enumerate(zip(sources, held))]
+        copies = [pltpu.make_async_copy(a, b, sem.at[n + i]) for i, (a, b) in enumerate(zip(held, results))]
+        for copy in taken:
             copy.start()
         me = lax.axis_index("dp") * lax.axis_size("fsdp") + lax.axis_index("fsdp")
 
@@ -1784,6 +1785,9 @@
         def row_of(x, i):
             return jnp.sum(jnp.where(iota(x.shape, 0) == i, x, 0.0), axis=0, keepdims=True)
 
+        for take, copy in zip(taken, copies):
+            take.wait()
+            copy.start()
         some = pick(early[...], me * e, e)
         down_b[...], gain_m[...], shift_m[...], out_b[...] = (some[i:i + 1] for i in range(4))
         some = pick(late[...], me * e, e)
@@ -1803,9 +1807,9 @@
     return pl.pallas_call(
         kernel,
         out_shape=[jax.ShapeDtypeStruct(a.shape, a.dtype) for a in whole] + [jax.ShapeDtypeStruct(s, F32) for s in small],
-        in_specs=[vm] * (3 + n),
+        in_specs=[vm] * 3 + [anyw] * n,
         out_specs=[anyw] * n + [vm] * len(small),
-        scratch_shapes=[pltpu.SemaphoreType.DMA((n,))],
+        scratch_shapes=[pltpu.VMEM(a.shape, a.dtype) for a in whole] + [pltpu.SemaphoreType.DMA((2 * n,))],
         name="finish",
     )(early, late, msum, *whole)
 

time: 233 us -> 233 us (level)
  no operation moved by 1% of the time
where the time goes in v4:
time: 233 us; the launch traced here: 230 us
  Pallas kernels  228 us (98%)
    pallas_call x1, Pallas kernels, forward_call(): pl.pallas_call(lambda *refs: forward_kernel(heads, devices, *refs), out_s...  144 us
    pallas_call x1, Pallas kernels, backward_call(): pl.pallas_call(lambda *refs: backward_kernel(heads, devices, *refs), out_...  78.4 us
    pallas_call x1, Pallas kernels, finish_call(): pl.pallas_call(kernel, out_shape=[jax.ShapeDtypeStruct(a.shape, a.dtype)...  4.94 us

profile of v4, /device:TPU:0, one launch (start us, length us, event | category | flops | bytes accessed | tf_op | source)
XLA Modules:
  0.0 230.0 jit_solution(5607151374972909571)
XLA Ops:
  0.6 1.5 pad_add_fusion.refs_6_
  2.2 144.2 %forward.1 = (bf16[768,1024]{1,0:T(8,128)(2,1)}, bf16[768,1024]{1,0:T(8,128)(2,1)}, bf16[1024,2304]{1,0:T(8,128)(2,1)}, bf16[1024,1536]{1,0:T(8,128)(2,1)}, bf16...) custom-call(s32[2]{0:T(128)} %refs_0_.1, ...), custom_call_target="tpu_custom_call" | custom-call | tf_op jit(solution)/shard_map/forward/pallas_call | solution.py:1106
  146.4 78.4 %backward.1 = (bf16[1024,768]{1,0:T(8,128)(2,1)}, f32[24,2304]{1,0:T(8,128)}, f32[24,768]{1,0:T(8,128)}, f32[24,3072]{1,0:T(8,128)}, f32[96,768]{1,0:T(8,128)}, ...) custom-call(bf16[1024,768]{1,0:T(8,128)(2,1)} %bitcast.22, bf16[768,1024]{1,0:T(8,128)(2,1)} %get-tuple-element.58.refs_1_, ...), custom_call_target="tpu_custom_call" | custom-call | tf_op jit(solution)/shard_map/backward/pallas_call | solution.py:1719
  224.8 4.9 %finish.1 = (bf16[1024,768]{1,0:T(8,128)(2,1)}, bf16[1024,768]{1,0:T(8,128)(2,1)}, f32[24,2304]{1,0:T(8,128)}, f32[24,768]{1,0:T(8,128)}, f32[24,3072]{1,0:T(8,1...) custom-call(f32[8,768]{1,0:T(8,128)} %get-tuple-element.75.refs_0_, ...), custom_call_target="tpu_custom_call" | custom-call | tf_op jit(solution)/shard_map/finish/pallas_call | solution.py:1807

commit v5 on v4

--- a/solution.py
+++ b/solution.py
@@ -1365,6 +1365,9 @@
         for i, (src, rows) in enumerate(pieces):
             self.s.go((self.name, 1), src, self.r1.at[:, :, :, rows, :], self.base + i, self.p.at(c=1 - self.p.c))
 
+    def core_columns(self, i, src, cols):
+        self.s.go((self.name, 1), src, self.r1.at[:, :, :, :, cols], self.base + (0, 1, 12)[i], self.p.at(c=1 - self.p.c))
+
     def second(self):
         p = self.p
         self.s.arrived((self.name, 1))
@@ -1623,8 +1626,9 @@
             low, high = y[..., :pieces], y[..., pieces:]
             keep, give = jnp.where(p.c == 0, low, high), jnp.where(p.c == 0, high, low)
             r.g[:, :, :, :, j * pieces:(j + 1) * pieces] = keep
-            away[i, :, :, :, :, j * pieces:(j + 1) * pieces] = give
-        r.core((away.at[i], slice(None)))
+            part = slice(j * pieces, (j + 1) * pieces)
+            away[i, :, :, :, :, part] = give
+            r.core_columns(j, away.at[i, :, :, :, :, part], part)
         if i == 2:
             sums["w"].start(0)
             bias_sums(width, gqkv, k_held.at[0, 8:10, :])

time: 233 us -> 238 us (1.021)
  Pallas kernels: 228 us -> 232 us
    pallas_call x1, Pallas kernels: 78.4 us -> 83.4 us  [backward_call(): pl.pallas_call(lambda *refs: backward_kernel(heads, devices, *refs), out_...]
where the time goes in v5:
time: 238 us; the launch traced here: 235 us
  Pallas kernels  232 us (97%)
    pallas_call x1, Pallas kernels, forward_call(): pl.pallas_call(lambda *refs: forward_kernel(heads, devices, *refs), out_s...  144 us
    pallas_call x1, Pallas kernels, backward_call(): pl.pallas_call(lambda *refs: backward_kernel(heads, devices, *refs), out_...  83.4 us
    pallas_call x1, Pallas kernels, finish_call(): pl.pallas_call(kernel, out_shape=[jax.ShapeDtypeStruct(a.shape, a.dtype)...  4.94 us

profile of v5, /device:TPU:0, one launch (start us, length us, event | category | flops | bytes accessed | tf_op | source)
XLA Modules:
  0.0 234.9 jit_solution(13866703630619223777)
XLA Ops:
  0.6 1.5 pad_add_fusion.refs_6_
  2.2 144.2 %forward.1 = (bf16[768,1024]{1,0:T(8,128)(2,1)}, bf16[768,1024]{1,0:T(8,128)(2,1)}, bf16[1024,2304]{1,0:T(8,128)(2,1)}, bf16[1024,1536]{1,0:T(8,128)(2,1)}, bf16...) custom-call(s32[2]{0:T(128)} %refs_0_.1, ...), custom_call_target="tpu_custom_call" | custom-call | tf_op jit(solution)/shard_map/forward/pallas_call | solution.py:1106
  146.4 83.4 %backward.1 = (bf16[1024,768]{1,0:T(8,128)(2,1)}, f32[24,2304]{1,0:T(8,128)}, f32[24,768]{1,0:T(8,128)}, f32[24,3072]{1,0:T(8,128)}, f32[96,768]{1,0:T(8,128)}, ...) custom-call(bf16[1024,768]{1,0:T(8,128)(2,1)} %bitcast.22, bf16[768,1024]{1,0:T(8,128)(2,1)} %get-tuple-element.58.refs_1_, ...), custom_call_target="tpu_custom_call" | custom-call | tf_op jit(solution)/shard_map/backward/pallas_call | solution.py:1723
  229.7 4.9 %finish.1 = (bf16[1024,768]{1,0:T(8,128)(2,1)}, bf16[1024,768]{1,0:T(8,128)(2,1)}, f32[24,2304]{1,0:T(8,128)}, f32[24,768]{1,0:T(8,128)}, f32[24,3072]{1,0:T(8,1...) custom-call(f32[8,768]{1,0:T(8,128)} %get-tuple-element.75.refs_0_, ...), custom_call_target="tpu_custom_call" | custom-call | tf_op jit(solution)/shard_map/finish/pallas_call | solution.py:1811
